TPU v7x, 32 devices: a whole 2x2x4 slice. The times are simulated.
32 devices in a mesh: blk: 8 (over y, x, core), exp: 4 (over z).
Axes of the slice: x: 2, y: 2, z: 4, core: 2. Of those that a mesh axis runs over, the one named last changes fastest.
Arguments:
- residual_deposit_sequence: bfloat16 [4, 1024, 1536], P('exp', 'blk'), may hold values from -60 to 60
- premix_rescaler: float32 [1536], replicated, may hold values from 0.25 to 1.75
- asking_projector: bfloat16 [1536, 1536], P(None, 'exp'), may hold values from -0.15625 to 0.15625
- lookup_projector: bfloat16 [1536, 512], P(None, 'exp'), may hold values from -0.15625 to 0.15625
- content_projector: bfloat16 [1536, 512], P(None, 'exp'), may hold values from -0.15625 to 0.15625
- final_projector: bfloat16 [1536, 1536], P('exp'), may hold values from -0.15625 to 0.15625
- logit_multipliers: float32 [12], replicated, may hold values from 1.5 to 6
- premixture_rescaler: float32 [1536], replicated, may hold values from 0.25 to 1.75
- specialist_switch_tensor: bfloat16 [8, 1536, 384], P('exp'), may hold values from -0.15625 to 0.15625
- specialist_widen_tensor: bfloat16 [8, 1536, 384], P('exp'), may hold values from -0.15625 to 0.15625
- specialist_shrink_tensor: bfloat16 [8, 384, 1536], P('exp'), may hold values from -0.3125 to 0.3125
- picked_specialist_labels: int32 [4, 1024, 2], P(None, 'blk'), may hold values from 0 to 7, all different within a row; in each aligned block of 128 rows (0 to 127, 128 to 255, ..., all dimensions but the last counted through in order) at most 64 rows name the same one
- specialist_shares: float32 [4, 1024, 2], P(None, 'blk'), may hold values from 0.1 to 1
Outputs:
- attention_update: bfloat16 [4, 1024, 1536], P('exp', 'blk')
- expert_update: bfloat16 [4, 1024, 1536], P('exp', 'blk')
Inputs may be any that keep to these rules, and one draw needn't show every extreme that they name: `picked_specialist_labels`: the 2 ids of a hit differ. Within each event's 128 hits on one index of blk (an aligned block of 128 rows) no expert is named by more than 64 hits, a bound that some block reaches.
All inputs are finite; a program needn't handle non-finite values.
Results may differ from a plain program's by a relative error of at most 0.019.
Values may be sent and summed in bfloat16 or wider, within the bound.
A program may use at most 192 MiB of HBM per device.

v0:
```python
import math

import jax
import jax.numpy as jnp
from jax import lax
from jax.sharding import PartitionSpec as P

D = 1536
PER_LANE_DIM = 128
TOP = 2
CAP = 64


def norm_rows(values, norm_gain):
    widened = values.astype(jnp.float32)
    return (
        widened * lax.rsqrt(jnp.mean(widened * widened, axis=-1, keepdims=True) + 1e-05) * norm_gain
    )


def head_norm(values):
    return values * lax.rsqrt(jnp.mean(values * values, axis=-1, keepdims=True) + 1e-06)


def attend_hits(
    rescaled_entries,
    asking_projector,
    lookup_projector,
    content_projector,
    final_projector,
    logit_multipliers,
):
    events, row_count, model_width = rescaled_entries.shape
    common_key_heads = lookup_projector.shape[1] // PER_LANE_DIM
    local_lane_count = asking_projector.shape[1] // PER_LANE_DIM
    askers_per_lookup = local_lane_count // common_key_heads
    query_heads = jnp.einsum(
        "std,de->ste", rescaled_entries, asking_projector, preferred_element_type=jnp.float32
    )
    query_heads = head_norm(
        query_heads.reshape(events, row_count, common_key_heads, askers_per_lookup, PER_LANE_DIM)
    ).astype(jnp.bfloat16)
    key_heads = jnp.einsum(
        "std,de->ste", rescaled_entries, lookup_projector, preferred_element_type=jnp.float32
    )
    key_heads = head_norm(
        key_heads.reshape(events, row_count, common_key_heads, PER_LANE_DIM)
    ).astype(jnp.bfloat16)
    value_heads = jnp.einsum(
        "std,de->ste", rescaled_entries, content_projector, preferred_element_type=jnp.float32
    )
    value_heads = value_heads.reshape(events, row_count, common_key_heads, PER_LANE_DIM).astype(
        jnp.bfloat16
    )
    inverse_root_dim = (logit_multipliers / math.sqrt(PER_LANE_DIM)).reshape(
        common_key_heads, askers_per_lookup
    )
    key_piece = lax.all_gather(key_heads, "blk", axis=1, tiled=True)
    value_piece = lax.all_gather(value_heads, "blk", axis=1, tiled=True)
    scores = jnp.einsum(
        "sikgd,sjkd->skgij", query_heads, key_piece, preferred_element_type=jnp.float32
    )
    expo = jnp.exp(scores * inverse_root_dim[None, :, :, None, None])
    totals = jnp.sum(expo, axis=-1)
    mixture = jnp.einsum(
        "skgij,sjkd->skgid",
        expo.astype(jnp.bfloat16),
        value_piece,
        preferred_element_type=jnp.float32,
    )
    totals, mixture = (totals, mixture)
    heads_out = head_norm(mixture / totals[..., None]).astype(jnp.bfloat16)
    out_blocks = final_projector.reshape(
        common_key_heads, askers_per_lookup, PER_LANE_DIM, model_width
    )
    return jnp.einsum("skgid,kgde->sie", heads_out, out_blocks, preferred_element_type=jnp.float32)


def slot_tables(chosen, expert_count):
    events, row_count, top_count = chosen.shape
    flat_ids = chosen.reshape(events, row_count * top_count)
    onehot = (
        flat_ids[:, :, None] == jnp.arange(expert_count, dtype=jnp.int32)[None, None, :]
    ).astype(jnp.int32)
    before = jnp.cumsum(onehot, axis=1) - onehot
    slot_of = jnp.sum(before * onehot, axis=2)
    source_rows = jnp.arange(row_count * top_count, dtype=jnp.int32)[None, :] // top_count
    event_index = jnp.arange(events, dtype=jnp.int32)[:, None]
    tables = (
        jnp.zeros((events, expert_count, CAP), jnp.int32)
        .at[event_index, flat_ids, slot_of]
        .set(source_rows)
    )
    return (slot_of, tables)


def run_experts(
    batched, specialist_switch_tensor, specialist_widen_tensor, specialist_shrink_tensor
):
    gate_act = jnp.einsum(
        "sjcd,jdf->sjcf", batched, specialist_switch_tensor, preferred_element_type=jnp.float32
    )
    up_act = jnp.einsum(
        "sjcd,jdf->sjcf", batched, specialist_widen_tensor, preferred_element_type=jnp.float32
    )
    hidden = (jax.nn.silu(gate_act) * up_act).astype(jnp.bfloat16)
    return jnp.einsum(
        "sjcf,jfd->sjcd", hidden, specialist_shrink_tensor, preferred_element_type=jnp.float32
    ).astype(jnp.bfloat16)


def body(
    residual_deposit_sequence,
    premix_rescaler,
    asking_projector,
    lookup_projector,
    content_projector,
    final_projector,
    logit_multipliers,
    premixture_rescaler,
    specialist_switch_tensor,
    specialist_widen_tensor,
    specialist_shrink_tensor,
    picked_specialist_labels,
    specialist_shares,
):
    specialist_slot = lax.axis_index("exp")
    exp_count = lax.axis_size("exp")
    rows_all = lax.all_gather(residual_deposit_sequence, "exp", axis=0, tiled=True)
    rescaled_entries = norm_rows(rows_all, premix_rescaler).astype(jnp.bfloat16)
    local_lane_count = asking_projector.shape[1] // PER_LANE_DIM
    device_scratch = lax.dynamic_slice_in_dim(
        logit_multipliers, specialist_slot * local_lane_count, local_lane_count
    )
    partial_out = attend_hits(
        rescaled_entries,
        asking_projector,
        lookup_projector,
        content_projector,
        final_projector,
        device_scratch,
    )
    attention_full = lax.psum_scatter(
        partial_out.astype(jnp.bfloat16), "exp", scatter_dimension=0, tiled=True
    ).astype(jnp.float32)
    attention_update = attention_full.astype(jnp.bfloat16)
    residual = residual_deposit_sequence.astype(jnp.float32) + attention_full
    expert_in = norm_rows(residual, premixture_rescaler).astype(jnp.bfloat16)
    row_count = expert_in.shape[1]
    local_experts = specialist_switch_tensor.shape[0]
    expert_count = local_experts * exp_count
    own_ids = lax.dynamic_slice_in_dim(picked_specialist_labels, specialist_slot, 1, 0)
    own_gates = lax.dynamic_slice_in_dim(specialist_shares, specialist_slot, 1, 0).reshape(
        row_count * TOP
    )
    slot_of, tables = slot_tables(own_ids, expert_count)
    outgoing = jnp.take(expert_in[0], tables[0].reshape(expert_count * CAP), axis=0)
    outgoing = outgoing.reshape(exp_count, local_experts, CAP, D)
    produced = run_experts(
        lax.all_to_all(outgoing, "exp", split_axis=0, concat_axis=0, tiled=True),
        specialist_switch_tensor,
        specialist_widen_tensor,
        specialist_shrink_tensor,
    )
    returned = lax.all_to_all(produced, "exp", split_axis=0, concat_axis=0, tiled=True)
    position = own_ids.reshape(row_count * TOP) * CAP + slot_of[0]
    values = jnp.take(returned.reshape(expert_count * CAP, D), position, axis=0).astype(jnp.float32)
    combined = jnp.sum((values * own_gates[:, None]).reshape(row_count, TOP, D), axis=1)
    expert_update = combined.astype(jnp.bfloat16)[None]
    return (attention_update, expert_update)


def solution(mesh):
    placed = (
        P("exp", "blk", None),
        P(),
        P(None, "exp"),
        P(None, "exp"),
        P(None, "exp"),
        P("exp", None),
        P(),
        P(),
        P("exp", None, None),
        P("exp", None, None),
        P("exp", None, None),
        P(None, "blk", None),
        P(None, "blk", None),
    )
    return jax.shard_map(
        body,
        mesh=mesh,
        in_specs=placed,
        out_specs=(P("exp", "blk", None), P("exp", "blk", None)),
        check_vma=False,
    )
```

profile of v0, /device:TPU:0, one launch (start us, length us, event | category | flops | bytes accessed | tf_op | source)
XLA Modules:
  0.0 258.9 jit_solution(3094345826512784104)
XLA Ops:
  7.2 0.7 all-gather.6.cloned.1.call-update
  8.0 41.4 %all-gather.6.cloned.1.call-done = bf16[4,128,1536]{2,1,0:T(8,128)(2,1)} async-done(((bf16[1,128,1536]{2,1,0:T(8,128)(2,1)}), bf16[4,128,1536]{2,1,0:T(8,128)(2,1)}) %all-gather.6.cloned.1.call-update) | async-done | bytes 1572880 | tf_op jit(solution)/shard_map/all_gather | solution.py:129
  49.4 1.9 fusion.1
  51.4 1.5 multiply_reduce_fusion.3
  52.9 0.7 multiply_convert_fusion.5
  53.7 2.7 %convolution_convert_fusion.1 = bf16[4,128,128]{2,1,0:T(8,128)(2,1)} fusion(bf16[4,128,1536]{2,1,0:T(8,128)(2,1)} %all-gather.6.cloned.1.call-done, f32[1536]{0:T(1024)S(1)} %copy-done.9, f32[4,128]{1,0:T(4,128)S(1)} %add_rsqrt_fusion.3, bf16[1536,128]{1,0:T(8,128)(2,1)S(1)} %copy-done.8), kind=kOutput, calls=%fused_computation.35 | convolution fusion | flops 204537856 | bytes 2105344 | tf_op jit(solution)/shard_map/std,de->ste/dot_general | solution.py:49
  56.4 0.0 reduce-scatter.2.cloned.1.call-start
  56.5 0.1 dynamic-slice_multiply_fusion
  56.6 3.7 %fusion.70 = (f32[4,128,384]{2,1,0:T(8,128)S(1)}, f32[4,128,384]{2,1,0:T(8,128)}) fusion(bf16[1536,384]{1,0:T(8,128)(2,1)} %param.15, bf16[4,128,1536]{2,1,0:T(8,128)(2,1)} %all-gather.6.cloned.1.call-done, f32[1536]{0:T(1024)S(1)} %copy-done.9, f32[4,128]{1,0:T(4,128)S(1)} %add_rsqrt_fusion.3), kind=kOutput, calls=%fused_computation.101 | convolution fusion | flops 607322112 | bytes 4333568 | tf_op jit(solution)/shard_map/std,de->ste/dot_general | solution.py:37
  60.2 1.1 copy.53
  61.4 1.4 copy.52
  62.8 1.2 reduce_sum.80
  64.0 12.2 %all-gather.8.cloned.1.call-done = bf16[4,1024,128]{1,2,0:T(8,128)(2,1)} async-done(((bf16[4,128,128]{1,2,0:T(8,128)(2,1)}), bf16[4,1024,128]{1,2,0:T(8,128)(2,1)}) %all-gather.8.cloned.1.call-update) | async-done | bytes 1048592 | tf_op jit(solution)/shard_map/all_gather | solution.py:58
  76.2 5.4 %bitcast_reduce_fusion = (f32[4,3,128]{2,1,0:T(4,128)S(1)}, f32[4,1024,128,3]{2,1,3,0:T(8,128)}) fusion(f32[3]{0:T(128)S(1)} %dynamic-slice_multiply_fusion, f32[4,128,3,128]{1,3,2,0:T(8,128)S(1)} %bitcast.150, f32[4,128,3]{1,2,0:T(4,128)S(1)} %add_rsqrt_fusion.1, bf16[4,1024,128]{1,2,0:T(8,128)(2,1)} %all-gather.8.cloned.1.call-done), kind=kOutput, calls=%fused_computation.3 | convolution fusion | flops 406190592 | bytes 8138764 | tf_op jit(solution)/shard_map/sikgd,sjkd->skgij/dot_general | solution.py:60
  81.6 20.6 %all-gather.10.cloned.1.call-done = bf16[4,1024,128]{2,1,0:T(8,128)(2,1)} async-done(((bf16[4,128,128]{2,1,0:T(8,128)(2,1)}), bf16[4,1024,128]{2,1,0:T(8,128)(2,1)}) %all-gather.10.cloned.1.call-update) | async-done | bytes 1048592 | tf_op jit(solution)/shard_map/all_gather | solution.py:59
  102.2 4.4 %multiply_reduce_fusion.2 = (f32[4,3,128]{2,1,0:T(4,128)S(1)}, f32[4,3,128,128]{2,3,1,0:T(8,128)S(1)}) fusion(f32[4,3,128]{2,1,0:T(4,128)S(1)} %get-tuple-element.8, bf16[4,1024,128]{2,1,0:T(8,128)(2,1)} %all-gather.10.cloned.1.call-done, f32[4,1024,128,3]{2,1,3,0:T(8,128)} %get-tuple-element.9, f32[3]{0:T(128)S(1)} %dynamic-slice_multiply_fusion), kind=kOutput, calls=%fused_computation.50 | convolution fusion | flops 406387200 | bytes 8138764 | tf_op jit(solution)/shard_map/skgij,sjkd->skgid/dot_general | solution.py:65
  106.7 2.2 fusion.8
  108.9 0.7 broadcast_multiply_fusion
  109.7 0.1 copy.59
  109.8 0.1 eq.27
  109.9 0.1 reshape.479
  110.1 0.6 reduce-window.6
  110.7 0.2 slice_reduce_fusion
  110.9 0.1 fusion.67
  111.1 11.2 %scatter_fusion = s32[8,64]{1,0:T(8,128)S(1)} fusion(s32[8,64]{1,0:T(8,128)S(1)} %broadcast.318, s32[256]{0:T(256)S(1)} %bitcast.148, s32[256]{0:T(256)S(1)} %bitcast.159), kind=kCustom, calls=%fused_computation.2 | custom fusion | bytes 5120 | tf_op jit(solution)/shard_map/scatter | solution.py:92
  122.3 0.1 reshape_squeeze.6
  122.4 22.0 %reduce-scatter.2.cloned.1.call-done = bf16[1,128,1536]{2,1,0:T(8,128)(2,1)} async-done(((bf16[4,128,1536]{2,1,0:T(8,128)(2,1)}), bf16[1,128,1536]{2,1,0:T(8,128)(2,1)}) %reduce-scatter.2.cloned.1.call-update) | async-done | bytes 393232 | tf_op jit(solution)/shard_map/reduce_scatter | solution.py:143
  144.3 1.2 multiply_reduce_fusion.1
  145.6 1.2 fusion.60
  146.7 3.0 %gather_fusion = bf16[512,1536]{1,0:T(8,128)(2,1)} fusion(bf16[128,1536]{1,0:T(8,128)(2,1)S(1)} %fusion.60, s32[1024]{0:T(1024)S(1)} %pad_clamp_fusion.1), kind=kCustom, calls=%fused_computation | custom fusion | bytes 3147776 | tf_op jit(solution)/shard_map/jit(_take)/gather | solution.py:157
  149.7 1.6 broadcast_select_fusion
  151.3 39.7 %all_to_all.10 = bf16[4,2,64,1536]{3,2,1,0:T(8,128)(2,1)S(1)} all-to-all(bf16[4,2,64,1536]{3,2,1,0:T(8,128)(2,1)S(1)} %broadcast_select_fusion), channel_id=1, replica_groups=mesh['blk'=8,'exp'=4] {'exp'}, dimensions={0} | all-to-all | bytes 3145728 | tf_op jit(solution)/shard_map/all_to_all | solution.py:160
  191.0 1.1 copy-done.3
  192.1 1.0 fusion.17
  193.2 5.1 %fusion.9 = bf16[4,2,64,1536]{3,2,0,1:T(8,128)(2,1)} fusion(bf16[2,384,1536]{2,1,0:T(8,128)(2,1)S(1)} %copy-done, bf16[2,1536,384]{2,1,0:T(8,128)(2,1)} %param.22, bf16[4,2,64,1536]{3,2,1,0:T(8,128)(2,1)} %copy-done.3, f32[4,2,64,384]{3,2,0,1:T(8,128)S(1)} %fusion.17), kind=kOutput, calls=%fused_computation.18 | convolution fusion | flops 1209925632 | bytes 8650752 | tf_op jit(solution)/shard_map/sjcf,jfd->sjcd/dot_general | solution.py:107
  198.3 2.7 %copy.65 = bf16[4,2,64,1536]{3,2,1,0:T(8,128)(2,1)} copy(bf16[4,2,64,1536]{3,2,0,1:T(8,128)(2,1)} %fusion.9) | data formatting | bytes 3145728 | tf_op jit(solution)/shard_map/convert_element_type | solution.py:109
  200.9 4.3 %all-to-all-start.1 = ((bf16[4,2,64,1536]{3,2,1,0:T(8,128)(2,1)}), bf16[4,2,64,1536]{3,2,1,0:T(8,128)(2,1)}, u32[]{:S(2)}, u32[]{:S(2)}) async-start(bf16[4,2,64,1536]{3,2,1,0:T(8,128)(2,1)} %copy.65), calls=%async_computation.2 | async-start | bytes 3145728 | tf_op jit(solution)/shard_map/all_to_all | solution.py:165
  205.3 0.1 reduce_sum.84
  205.4 0.1 copy.66
  205.5 0.1 mul.173
  205.7 0.7 dynamic-slice_bitcast_fusion
  206.3 0.1 copy.67
  206.5 0.1 copy.60
  206.5 0.1 copy.61
  206.7 35.1 %all-to-all-done.1 = bf16[4,2,64,1536]{3,2,1,0:T(8,128)(2,1)} async-done(((bf16[4,2,64,1536]{3,2,1,0:T(8,128)(2,1)}), bf16[4,2,64,1536]{3,2,1,0:T(8,128)(2,1)}, u32[]{:S(2)}, u32[]{:S(2)}) %all-to-all-start.1) | async-done | bytes 1572896 | tf_op jit(solution)/shard_map/all_to_all | solution.py:165
  241.8 4.5 %gather_fusion.1 = bf16[256,1536]{1,0:T(8,128)(2,1)} fusion(bf16[512,1536]{1,0:T(8,128)(2,1)} %bitcast.38, s32[1024]{0:T(1024)S(1)} %pad_clamp_fusion), kind=kCustom, calls=%fused_computation.1 | custom fusion | bytes 1573888 | tf_op jit(solution)/shard_map/jit(_take)/gather | solution.py:167
  246.3 2.2 gather.15
  248.4 3.9 %multiply_reduce_fusion = bf16[128,1536]{1,0:T(8,128)(2,1)} fusion(bf16[128,2,1536]{2,1,0:T(2,128)(2,1)S(1)} %gather.15, pred[128,2]{1,0:T(8,128)(4,1)S(1)} %copy.61, f32[128,2]{1,0:T(8,128)S(1)} %copy.67), kind=kLoop, calls=%fused_computation.24 | loop fusion | flops 1376256 | bytes 1180928 | tf_op jit(solution)/shard_map/reduce_sum | solution.py:168
  (47 shorter events, 0.4 us)
Async XLA Ops:
  7.2 186.0 %copy-start = (bf16[2,384,1536]{2,1,0:T(8,128)(2,1)S(1)}, bf16[2,384,1536]{2,1,0:T(8,128)(2,1)}, u32[]{:S(2)}) copy-start(bf16[2,384,1536]{2,1,0:T(8,128)(2,1)} %param.23) | copy-start | bytes 7077892
  7.2 44.2 %copy-start.7 = (bf16[1536,128]{1,0:T(8,128)(2,1)S(1)}, bf16[1536,128]{1,0:T(8,128)(2,1)}, u32[]{:S(2)}) copy-start(bf16[1536,128]{1,0:T(8,128)(2,1)} %param.16) | copy-start | bytes 1179652
  7.2 42.2 %all-gather.6.cloned.1.call-start = ((), (), s32[]{:S(2)}) async-start(), calls=%async_computation.3 | async-start | bytes 1966080 | tf_op jit(solution)/shard_map/all_gather | solution.py:129
  7.9 68.3 %all-gather.8.cloned.1.call-start = ((), (), s32[]{:S(2)}) async-start(), calls=%async_computation.5 | async-start | bytes 1179648 | tf_op jit(solution)/shard_map/all_gather | solution.py:58
  49.4 1.9 copy-start.2
  51.4 2.3 copy-start.8
  51.4 2.3 copy-start.9
  53.6 2.9 %copy-start.10 = (f32[12]{0:T(128)S(1)}, f32[12]{0:T(128)}, u32[]{:S(2)}) copy-start(f32[12]{0:T(128)} %param.19) | copy-start | bytes 148
  53.6 48.6 %all-gather.10.cloned.1.call-start = ((), (), s32[]{:S(2)}) async-start(), calls=%async_computation.6 | async-start | bytes 1179648 | tf_op jit(solution)/shard_map/all_gather | solution.py:59
  56.4 87.9 %reduce-scatter.2.cloned.1.call-start = ((), (), s32[]{:S(2)}) async-start(), calls=%async_computation.4 | async-start | bytes 1966080 | tf_op jit(solution)/shard_map/reduce_scatter | solution.py:143
  102.2 4.5 %copy-start.4 = (bf16[384,1536]{1,0:T(8,128)(2,1)S(1)}, bf16[384,1536]{1,0:T(8,128)(2,1)}, u32[]{:S(2)}) copy-start(bf16[384,1536]{1,0:T(8,128)(2,1)} %param.18) | copy-start | bytes 3538948
  108.9 35.4 %copy-start.1 = (bf16[1,128,1536]{2,1,0:T(8,128)(2,1)S(1)}, bf16[1,128,1536]{2,1,0:T(8,128)(2,1)}, u32[]{:S(2)}) copy-start(bf16[1,128,1536]{2,1,0:T(8,128)(2,1)} %param.13) | copy-start | bytes 1179652
  110.0 35.5 %copy-start.5 = (f32[1536]{0:T(1024)S(1)}, f32[1536]{0:T(1024)}, u32[]{:S(2)}) copy-start(f32[1536]{0:T(1024)} %param.20) | copy-start | bytes 18436
  151.3 40.8 %copy-start.6 = (bf16[2,1536,384]{2,1,0:T(8,128)(2,1)S(1)}, bf16[2,1536,384]{2,1,0:T(8,128)(2,1)}, u32[]{:S(2)}) copy-start(bf16[2,1536,384]{2,1,0:T(8,128)(2,1)} %param.21) | copy-start | bytes 7077892
  191.0 1.1 copy-start.3
  200.9 40.9 %all-to-all-start.1 = ((bf16[4,2,64,1536]{3,2,1,0:T(8,128)(2,1)}), bf16[4,2,64,1536]{3,2,1,0:T(8,128)(2,1)}, u32[]{:S(2)}, u32[]{:S(2)}) async-start(bf16[4,2,64,1536]{3,2,1,0:T(8,128)(2,1)} %copy.65), calls=%async_computation.2 | async-start | bytes 3145728 | tf_op jit(solution)/shard_map/all_to_all | solution.py:165
Sparse Core Ops, SparseCore 0:
  9.6 39.7 all-gather.5
  53.8 22.4 all-gather.7
  78.7 23.4 all-gather.9
  109.0 35.2 reduce-scatter.1
where the time goes:
time: 260 us; the launch traced here: 259 us
  waiting for transfers between devices  132 us (51%)
  blocking collectives  39.7 us (15%)
  local copies, waits for them, and re-layouts  29.3 us (11%)
  matrix products  26 us (10%)
  between operations  14.1 us (5%)
  other arithmetic  13.3 us (5%)
  starting transfers between devices  4.49 us (2%)
    all_gather x1, waiting for transfers between devices, body(): lax.all_gather(residual_deposit_sequence, 'exp', axis=0, tiled=True)  41.4 us
    all_to_all x1, blocking collectives, body(): lax.all_to_all(outgoing, 'exp', split_axis=0, concat_axis=0, tiled=True)  39.7 us
    all_to_all x1, waiting for transfers between devices, body(): lax.all_to_all(produced, 'exp', split_axis=0, concat_axis=0, tiled=True)  35.1 us
    reduce_scatter x1, waiting for transfers between devices, body(): lax.psum_scatter(partial_out.astype(jnp.bfloat16), 'exp', scatter_dimensi...  22 us
    all_gather x1, waiting for transfers between devices, attend_hits(): value_piece = lax.all_gather(value_heads, 'blk', axis=1, tiled=True)  20.6 us
    all_gather x1, waiting for transfers between devices, attend_hits(): key_piece = lax.all_gather(key_heads, 'blk', axis=1, tiled=True)  12.2 us
    scatter x1, local copies, waits for them, and re-layouts, slot_tables(): tables = jnp.zeros((events, expert_count, CAP), jnp.int32).at[event_index...  11.2 us
    gather x2, local copies, waits for them, and re-layouts, body(): jnp.take(returned.reshape(expert_count * CAP, D), position, axis=0)  6.65 us
  transfers between devices with their start and end apart: 5, of which 5 were waited for; matrix products, arithmetic and copies ran while one was open for 12% of the time, Pallas kernels for 0%

commit v1 on v0

--- a/solution.py
+++ b/solution.py
@@ -76,37 +76,16 @@
     return jnp.einsum("skgid,kgde->sie", heads_out, out_blocks, preferred_element_type=jnp.float32)
 
 
-def slot_tables(chosen, expert_count):
-    events, row_count, top_count = chosen.shape
-    flat_ids = chosen.reshape(events, row_count * top_count)
-    onehot = (
-        flat_ids[:, :, None] == jnp.arange(expert_count, dtype=jnp.int32)[None, None, :]
-    ).astype(jnp.int32)
-    before = jnp.cumsum(onehot, axis=1) - onehot
-    slot_of = jnp.sum(before * onehot, axis=2)
-    source_rows = jnp.arange(row_count * top_count, dtype=jnp.int32)[None, :] // top_count
-    event_index = jnp.arange(events, dtype=jnp.int32)[:, None]
-    tables = (
-        jnp.zeros((events, expert_count, CAP), jnp.int32)
-        .at[event_index, flat_ids, slot_of]
-        .set(source_rows)
-    )
-    return (slot_of, tables)
+def gates_of(labels, shares, expert_ids):
+    hit = labels[..., None, :] == expert_ids[:, None]
+    return jnp.sum(jnp.where(hit, shares[..., None, :], 0.0), axis=-1)
 
 
-def run_experts(
-    batched, specialist_switch_tensor, specialist_widen_tensor, specialist_shrink_tensor
-):
-    gate_act = jnp.einsum(
-        "sjcd,jdf->sjcf", batched, specialist_switch_tensor, preferred_element_type=jnp.float32
-    )
-    up_act = jnp.einsum(
-        "sjcd,jdf->sjcf", batched, specialist_widen_tensor, preferred_element_type=jnp.float32
-    )
-    hidden = (jax.nn.silu(gate_act) * up_act).astype(jnp.bfloat16)
-    return jnp.einsum(
-        "sjcf,jfd->sjcd", hidden, specialist_shrink_tensor, preferred_element_type=jnp.float32
-    ).astype(jnp.bfloat16)
+def run_experts(rows, gates, switch, widen, shrink):
+    gate_act = jnp.einsum("td,jdf->tjf", rows, switch, preferred_element_type=jnp.float32)
+    up_act = jnp.einsum("td,jdf->tjf", rows, widen, preferred_element_type=jnp.float32)
+    hidden = (jax.nn.silu(gate_act) * up_act * gates[:, :, None]).astype(jnp.bfloat16)
+    return jnp.einsum("tjf,jfd->td", hidden, shrink, preferred_element_type=jnp.float32)
 
 
 def body(
@@ -146,27 +125,21 @@
     attention_update = attention_full.astype(jnp.bfloat16)
     residual = residual_deposit_sequence.astype(jnp.float32) + attention_full
     expert_in = norm_rows(residual, premixture_rescaler).astype(jnp.bfloat16)
-    row_count = expert_in.shape[1]
     local_experts = specialist_switch_tensor.shape[0]
-    expert_count = local_experts * exp_count
-    own_ids = lax.dynamic_slice_in_dim(picked_specialist_labels, specialist_slot, 1, 0)
-    own_gates = lax.dynamic_slice_in_dim(specialist_shares, specialist_slot, 1, 0).reshape(
-        row_count * TOP
-    )
-    slot_of, tables = slot_tables(own_ids, expert_count)
-    outgoing = jnp.take(expert_in[0], tables[0].reshape(expert_count * CAP), axis=0)
-    outgoing = outgoing.reshape(exp_count, local_experts, CAP, D)
-    produced = run_experts(
-        lax.all_to_all(outgoing, "exp", split_axis=0, concat_axis=0, tiled=True),
+    expert_ids = specialist_slot * local_experts + jnp.arange(local_experts, dtype=jnp.int32)
+    gates = gates_of(picked_specialist_labels, specialist_shares, expert_ids)
+    rows = lax.all_gather(expert_in, "exp", axis=0, tiled=True)
+    events, row_count, _ = rows.shape
+    summed = run_experts(
+        rows.reshape(events * row_count, D),
+        gates.reshape(events * row_count, local_experts),
         specialist_switch_tensor,
         specialist_widen_tensor,
         specialist_shrink_tensor,
+    ).astype(jnp.bfloat16)
+    expert_update = lax.psum_scatter(
+        summed.reshape(events, row_count, D), "exp", scatter_dimension=0, tiled=True
     )
-    returned = lax.all_to_all(produced, "exp", split_axis=0, concat_axis=0, tiled=True)
-    position = own_ids.reshape(row_count * TOP) * CAP + slot_of[0]
-    values = jnp.take(returned.reshape(expert_count * CAP, D), position, axis=0).astype(jnp.float32)
-    combined = jnp.sum((values * own_gates[:, None]).reshape(row_count, TOP, D), axis=1)
-    expert_update = combined.astype(jnp.bfloat16)[None]
     return (attention_update, expert_update)
 
 

time: 260 us -> 237 us (0.912)
  waiting for transfers between devices: 132 us -> 181 us
  blocking collectives: 39.7 us -> 0 us
  local copies, waits for them, and re-layouts: 29.3 us -> 2.62 us
  other arithmetic: 13.3 us -> 7.1 us
  matrix products: 26 us -> 31.5 us
  starting transfers between devices: 4.49 us -> 0.24 us
    all_to_all x1 -> x0, blocking collectives: 39.7 us -> none  [body(): lax.all_to_all(outgoing, 'exp', split_axis=0, concat_axis=0, tiled=True)]
    all_gather x0 -> x1, waiting for transfers between devices: none -> 36 us  [body(): rows = lax.all_gather(expert_in, 'exp', axis=0, tiled=True)]
    all_to_all x1 -> x0, waiting for transfers between devices: 35.1 us -> none  [body(): lax.all_to_all(produced, 'exp', split_axis=0, concat_axis=0, tiled=True)]
    reduce_scatter x0 -> x1, waiting for transfers between devices: none -> 34.3 us  [body(): lax.psum_scatter(summed.reshape(events, row_count, D), 'exp', scatter_dim...]
    reduce_scatter x1, waiting for transfers between devices: 22 us -> 35.4 us  [body(): lax.psum_scatter(partial_out.astype(jnp.bfloat16), 'exp', scatter_dimensi...]
    scatter x1 -> x0, local copies, waits for them, and re-layouts: 11.2 us -> none  [slot_tables(): tables = jnp.zeros((events, expert_count, CAP), jnp.int32).at[event_index...]
    gather x3 -> x0, local copies, waits for them, and re-layouts: 9.61 us -> none  [the longest x2 6.65 us: body(): jnp.take(returned.reshape(expert_count * CAP, D), position, axis=0)]
    dot_general x2, matrix products: 6.11 us -> 11.6 us  [the longest x1 6.9 us: run_experts(): jnp.einsum('tjf,jfd->td', hidden, shrink, preferred_element_type=jnp.floa...]
  transfers between devices with their start and end apart: 5 -> 6, of which waited for: 5 -> 6; matrix products, arithmetic and copies ran while one was open for 12% -> 7% of each run, Pallas kernels for 0% -> 0%
where the time goes in v1:
time: 237 us; the launch traced here: 236 us
  waiting for transfers between devices  181 us (76%)
  matrix products  31.5 us (13%)
  between operations  14.3 us (6%)
  other arithmetic  7.1 us (3%)
  local copies, waits for them, and re-layouts  2.62 us (1%)
    all_gather x1, waiting for transfers between devices, body(): lax.all_gather(residual_deposit_sequence, 'exp', axis=0, tiled=True)  41.4 us
    all_gather x1, waiting for transfers between devices, body(): rows = lax.all_gather(expert_in, 'exp', axis=0, tiled=True)  36 us
    reduce_scatter x1, waiting for transfers between devices, body(): lax.psum_scatter(partial_out.astype(jnp.bfloat16), 'exp', scatter_dimensi...  35.4 us
    reduce_scatter x1, waiting for transfers between devices, body(): lax.psum_scatter(summed.reshape(events, row_count, D), 'exp', scatter_dim...  34.3 us
    all_gather x1, waiting for transfers between devices, attend_hits(): value_piece = lax.all_gather(value_heads, 'blk', axis=1, tiled=True)  20.6 us
    all_gather x1, waiting for transfers between devices, attend_hits(): key_piece = lax.all_gather(key_heads, 'blk', axis=1, tiled=True)  12.2 us
    dot_general x1, matrix products, run_experts(): jnp.einsum('tjf,jfd->td', hidden, shrink, preferred_element_type=jnp.floa...  6.9 us
    dot_general x1, matrix products, attend_hits(): jnp.einsum('sikgd,sjkd->skgij', query_heads, key_piece, preferred_element...  5.4 us
  transfers between devices with their start and end apart: 6, of which 6 were waited for; matrix products, arithmetic and copies ran while one was open for 7% of the time, Pallas kernels for 0%

profile of v1, /device:TPU:0, one launch (start us, length us, event | category | flops | bytes accessed | tf_op | source)
XLA Modules:
  0.0 236.5 jit_solution(15688548943295369664)
XLA Ops:
  7.2 0.0 copy-start
  7.2 0.0 copy-start.7
  7.2 0.0 all-gather.7.cloned.1.call-start
  7.2 0.7 all-gather.7.cloned.1.call-update
  7.9 0.0 all-gather.11.cloned.1.call-start
  8.0 41.4 %all-gather.7.cloned.1.call-done = bf16[4,128,1536]{2,1,0:T(8,128)(2,1)} async-done(((bf16[1,128,1536]{2,1,0:T(8,128)(2,1)}), bf16[4,128,1536]{2,1,0:T(8,128)(2,1)}) %all-gather.7.cloned.1.call-update) | async-done | bytes 1572880 | tf_op jit(solution)/shard_map/all_gather | solution.py:108
  49.4 1.9 fusion.1
  51.3 0.0 copy-done.7
  51.3 0.0 copy-done.2
  51.4 0.0 copy-start.8
  51.4 0.0 copy-start.9
  51.4 1.5 multiply_reduce_fusion.2
  52.9 0.7 multiply_convert_fusion.6
  53.6 0.0 all-gather.11.cloned.1.call-update
  53.6 0.0 copy-start.10
  53.6 0.0 all-gather.13.cloned.1.call-start
  53.7 0.0 copy-done.8
  53.7 0.0 copy-done.9
  53.7 2.7 %convolution_convert_fusion = bf16[4,128,128]{2,1,0:T(8,128)(2,1)} fusion(bf16[4,128,1536]{2,1,0:T(8,128)(2,1)} %all-gather.7.cloned.1.call-done, f32[1536]{0:T(1024)S(1)} %copy-done.9, f32[4,128]{1,0:T(4,128)S(1)} %add_rsqrt_fusion.3, bf16[1536,128]{1,0:T(8,128)(2,1)S(1)} %copy-done.8), kind=kOutput, calls=%fused_computation.19 | convolution fusion | flops 204537856 | bytes 2105344 | tf_op jit(solution)/shard_map/std,de->ste/dot_general | solution.py:49
  56.4 0.0 all-gather.13.cloned.1.call-update
  56.4 0.0 reduce-scatter.3.cloned.1.call-start
  56.5 0.0 copy-done.10
  56.5 0.1 dynamic-slice_multiply_fusion
  56.6 3.7 %fusion.31 = (f32[4,128,384]{2,1,0:T(8,128)S(1)}, f32[4,128,384]{2,1,0:T(8,128)}) fusion(bf16[1536,384]{1,0:T(8,128)(2,1)} %param.15, bf16[4,128,1536]{2,1,0:T(8,128)(2,1)} %all-gather.7.cloned.1.call-done, f32[1536]{0:T(1024)S(1)} %copy-done.9, f32[4,128]{1,0:T(4,128)S(1)} %add_rsqrt_fusion.3), kind=kOutput, calls=%fused_computation.49 | convolution fusion | flops 607322112 | bytes 4333568 | tf_op jit(solution)/shard_map/std,de->ste/dot_general | solution.py:37
  60.2 1.2 copy.43
  61.4 1.4 copy.42
  62.8 1.2 reduce_sum.65
  64.0 12.2 %all-gather.11.cloned.1.call-done = bf16[4,1024,128]{1,2,0:T(8,128)(2,1)} async-done(((bf16[4,128,128]{1,2,0:T(8,128)(2,1)}), bf16[4,1024,128]{1,2,0:T(8,128)(2,1)}) %all-gather.11.cloned.1.call-update) | async-done | bytes 1048592 | tf_op jit(solution)/shard_map/all_gather | solution.py:58
  76.2 5.4 %bitcast_reduce_fusion = (f32[4,3,128]{2,1,0:T(4,128)S(1)}, f32[4,1024,128,3]{2,1,3,0:T(8,128)}) fusion(f32[3]{0:T(128)S(1)} %dynamic-slice_multiply_fusion, f32[4,128,3,128]{1,3,2,0:T(8,128)S(1)} %bitcast.91, f32[4,128,3]{1,2,0:T(4,128)S(1)} %add_rsqrt_fusion.1, bf16[4,1024,128]{1,2,0:T(8,128)(2,1)} %all-gather.11.cloned.1.call-done), kind=kOutput, calls=%fused_computation | convolution fusion | flops 406190592 | bytes 8138764 | tf_op jit(solution)/shard_map/sikgd,sjkd->skgij/dot_general | solution.py:60
  81.6 20.6 %all-gather.13.cloned.1.call-done = bf16[4,1024,128]{2,1,0:T(8,128)(2,1)} async-done(((bf16[4,128,128]{2,1,0:T(8,128)(2,1)}), bf16[4,1024,128]{2,1,0:T(8,128)(2,1)}) %all-gather.13.cloned.1.call-update) | async-done | bytes 1048592 | tf_op jit(solution)/shard_map/all_gather | solution.py:59
  102.2 4.4 %multiply_reduce_fusion.1 = (f32[4,3,128]{2,1,0:T(4,128)S(1)}, f32[4,3,128,128]{2,3,1,0:T(8,128)S(1)}) fusion(f32[4,3,128]{2,1,0:T(4,128)S(1)} %get-tuple-element.6, bf16[4,1024,128]{2,1,0:T(8,128)(2,1)} %all-gather.13.cloned.1.call-done, f32[4,1024,128,3]{2,1,3,0:T(8,128)} %get-tuple-element.7, f32[3]{0:T(128)S(1)} %dynamic-slice_multiply_fusion), kind=kOutput, calls=%fused_computation.31 | convolution fusion | flops 406387200 | bytes 8138764 | tf_op jit(solution)/shard_map/skgij,sjkd->skgid/dot_general | solution.py:65
  106.7 2.2 fusion.8
  108.9 0.0 reduce-scatter.3.cloned.1.call-update
  108.9 0.0 copy-start.5
  108.9 0.0 copy-start.6
  108.9 0.0 all-gather.9.cloned.1.call-start
  109.0 35.4 %reduce-scatter.3.cloned.1.call-done = bf16[1,128,1536]{2,1,0:T(8,128)(2,1)} async-done(((bf16[4,128,1536]{2,1,0:T(8,128)(2,1)}), bf16[1,128,1536]{2,1,0:T(8,128)(2,1)}) %reduce-scatter.3.cloned.1.call-update) | async-done | bytes 393232 | tf_op jit(solution)/shard_map/reduce_scatter | solution.py:122
  144.4 1.2 multiply_reduce_fusion
  145.6 1.9 multiply_convert_fusion.1
  147.5 0.0 all-gather.9.cloned.1.call-update
  147.5 0.0 reduce-scatter.5.cloned.1.call-start
  147.6 0.0 copy-done.6
  147.6 0.1 select_reduce_fusion
  147.7 36.0 %all-gather.9.cloned.1.call-done = bf16[4,128,1536]{2,1,0:T(8,128)(2,1)} async-done(((bf16[1,128,1536]{2,1,0:T(8,128)(2,1)}), bf16[4,128,1536]{2,1,0:T(8,128)(2,1)}) %all-gather.9.cloned.1.call-update) | async-done | bytes 1572880 | tf_op jit(solution)/shard_map/all_gather | solution.py:131
  183.7 4.7 %fusion.32 = f32[512,2,384]{2,0,1:T(8,128)} fusion(bf16[512,1536,1]{1,0,2:T(8,128)(2,1)} %bitcast.97, bf16[2,1536,384]{2,1,0:T(8,128)(2,1)} %param.21), kind=kOutput, calls=%fused_computation.50 | convolution fusion | flops 1207959552 | bytes 5505024 | tf_op jit(solution)/shard_map/td,jdf->tjf/dot_general | solution.py:85
  188.4 6.9 %fusion.9 = bf16[512,1536]{1,0:T(8,128)(2,1)} fusion(bf16[2,384,1536]{2,1,0:T(8,128)(2,1)S(1)} %copy-done, f32[512,2,384]{2,0,1:T(8,128)} %fusion.32, bf16[512,1536,1]{1,0,2:T(8,128)(2,1)} %bitcast.98, bf16[2,1536,384]{2,1,0:T(8,128)(2,1)} %param.22, f32[512,2]{0,1:T(2,128)S(1)} %bitcast.96), kind=kOutput, calls=%fused_computation.15 | convolution fusion | flops 2419458048 | bytes 9441280 | tf_op jit(solution)/shard_map/tjf,jfd->td/dot_general | solution.py:88
  195.3 0.0 reduce-scatter.5.cloned.1.call-update
  195.3 34.3 %reduce-scatter.5.cloned.1.call-done = bf16[1,128,1536]{2,1,0:T(8,128)(2,1)} async-done(((bf16[4,128,1536]{2,1,0:T(8,128)(2,1)}), bf16[1,128,1536]{2,1,0:T(8,128)(2,1)}) %reduce-scatter.5.cloned.1.call-update) | async-done | bytes 393232 | tf_op jit(solution)/shard_map/reduce_scatter | solution.py:140
  (18 shorter events, 0.1 us)
Async XLA Ops:
  7.2 181.2 %copy-start = (bf16[2,384,1536]{2,1,0:T(8,128)(2,1)S(1)}, bf16[2,384,1536]{2,1,0:T(8,128)(2,1)}, u32[]{:S(2)}) copy-start(bf16[2,384,1536]{2,1,0:T(8,128)(2,1)} %param.23) | copy-start | bytes 7077892
  7.2 44.2 %copy-start.7 = (bf16[1536,128]{1,0:T(8,128)(2,1)S(1)}, bf16[1536,128]{1,0:T(8,128)(2,1)}, u32[]{:S(2)}) copy-start(bf16[1536,128]{1,0:T(8,128)(2,1)} %param.16) | copy-start | bytes 1179652
  7.2 42.2 %all-gather.7.cloned.1.call-start = ((), (), s32[]{:S(2)}) async-start(), calls=%async_computation.2 | async-start | bytes 1966080 | tf_op jit(solution)/shard_map/all_gather | solution.py:108
  7.9 68.3 %all-gather.11.cloned.1.call-start = ((), (), s32[]{:S(2)}) async-start(), calls=%async_computation.6 | async-start | bytes 1179648 | tf_op jit(solution)/shard_map/all_gather | solution.py:58
  49.4 1.9 copy-start.2
  51.4 2.3 copy-start.8
  51.4 2.3 copy-start.9
  53.6 2.9 %copy-start.10 = (f32[12]{0:T(128)S(1)}, f32[12]{0:T(128)}, u32[]{:S(2)}) copy-start(f32[12]{0:T(128)} %param.19) | copy-start | bytes 148
  53.6 48.6 %all-gather.13.cloned.1.call-start = ((), (), s32[]{:S(2)}) async-start(), calls=%async_computation.7 | async-start | bytes 1179648 | tf_op jit(solution)/shard_map/all_gather | solution.py:59
  56.4 87.9 %reduce-scatter.3.cloned.1.call-start = ((), (), s32[]{:S(2)}) async-start(), calls=%async_computation.3 | async-start | bytes 1966080 | tf_op jit(solution)/shard_map/reduce_scatter | solution.py:122
  102.2 4.5 %copy-start.3 = (bf16[384,1536]{1,0:T(8,128)(2,1)S(1)}, bf16[384,1536]{1,0:T(8,128)(2,1)}, u32[]{:S(2)}) copy-start(bf16[384,1536]{1,0:T(8,128)(2,1)} %param.18) | copy-start | bytes 3538948
  108.9 35.5 %copy-start.1 = (bf16[1,128,1536]{2,1,0:T(8,128)(2,1)S(1)}, bf16[1,128,1536]{2,1,0:T(8,128)(2,1)}, u32[]{:S(2)}) copy-start(bf16[1,128,1536]{2,1,0:T(8,128)(2,1)} %param.13) | copy-start | bytes 1179652
  108.9 36.7 %copy-start.4 = (f32[1536]{0:T(1024)S(1)}, f32[1536]{0:T(1024)}, u32[]{:S(2)}) copy-start(f32[1536]{0:T(1024)} %param.20) | copy-start | bytes 18436
  108.9 38.6 %copy-start.5 = (s32[4,128,2]{1,2,0:T(2,128)S(1)}, s32[4,128,2]{1,2,0:T(2,128)}, u32[]{:S(2)}) copy-start(s32[4,128,2]{1,2,0:T(2,128)} %param.24) | copy-start | bytes 12292
  108.9 38.7 %copy-start.6 = (f32[4,128,2]{1,2,0:T(2,128)S(1)}, f32[4,128,2]{1,2,0:T(2,128)}, u32[]{:S(2)}) copy-start(f32[4,128,2]{1,2,0:T(2,128)} %param.25) | copy-start | bytes 12292
  108.9 74.8 %all-gather.9.cloned.1.call-start = ((), (), s32[]{:S(2)}) async-start(), calls=%async_computation.4 | async-start | bytes 1966080 | tf_op jit(solution)/shard_map/all_gather | solution.py:131
  147.5 82.1 %reduce-scatter.5.cloned.1.call-start = ((), (), s32[]{:S(2)}) async-start(), calls=%async_computation.5 | async-start | bytes 1966080 | tf_op jit(solution)/shard_map/reduce_scatter | solution.py:140
Sparse Core Ops, SparseCore 0:
  9.6 39.7 all-gather.6
  53.8 22.4 all-gather.10
  78.7 23.4 all-gather.12
  109.0 35.2 reduce-scatter.2
  147.6 36.0 all-gather.8
  195.4 34.1 reduce-scatter.4

commit v2 on v1

--- a/solution.py
+++ b/solution.py
@@ -1,8 +1,11 @@
+import functools
 import math
 
 import jax
 import jax.numpy as jnp
 from jax import lax
+from jax.experimental import pallas as pl
+from jax.experimental.pallas import tpu as pltpu
 from jax.sharding import PartitionSpec as P
 
 D = 1536
@@ -55,8 +58,10 @@
     inverse_root_dim = (logit_multipliers / math.sqrt(PER_LANE_DIM)).reshape(
         common_key_heads, askers_per_lookup
     )
-    key_piece = lax.all_gather(key_heads, "blk", axis=1, tiled=True)
-    value_piece = lax.all_gather(value_heads, "blk", axis=1, tiled=True)
+    pair = lax.all_gather(
+        jnp.concatenate([key_heads, value_heads], axis=-1), "blk", axis=1, tiled=True
+    )
+    key_piece, value_piece = pair[..., :PER_LANE_DIM], pair[..., PER_LANE_DIM:]
     scores = jnp.einsum(
         "sikgd,sjkd->skgij", query_heads, key_piece, preferred_element_type=jnp.float32
     )
@@ -81,11 +86,133 @@
     return jnp.sum(jnp.where(hit, shares[..., None, :], 0.0), axis=-1)
 
 
-def run_experts(rows, gates, switch, widen, shrink):
-    gate_act = jnp.einsum("td,jdf->tjf", rows, switch, preferred_element_type=jnp.float32)
-    up_act = jnp.einsum("td,jdf->tjf", rows, widen, preferred_element_type=jnp.float32)
-    hidden = (jax.nn.silu(gate_act) * up_act * gates[:, :, None]).astype(jnp.bfloat16)
-    return jnp.einsum("tjf,jfd->td", hidden, shrink, preferred_element_type=jnp.float32)
+def greet_all(n, axis):
+    me = lax.axis_index(axis)
+    barrier = pltpu.get_barrier_semaphore()
+
+    @pl.loop(1, n)
+    def _(k):
+        pl.semaphore_signal(
+            barrier,
+            inc=1,
+            device_id={axis: lax.rem(me + k, n)},
+            device_id_type=pl.DeviceIdType.MESH,
+        )
+
+    pl.semaphore_wait(barrier, n - 1)
+
+
+def copy_to(src, dst, send_sem, recv_sem, **where):
+    return pltpu.make_async_remote_copy(
+        src_ref=src,
+        dst_ref=dst,
+        send_sem=send_sem,
+        recv_sem=recv_sem,
+        device_id=where,
+        device_id_type=pl.DeviceIdType.MESH,
+    )
+
+
+def line_sends(n, me, s, block, held, up_sem, down_sem, recv_sem):
+    up = copy_to(block, held.at[s], up_sem.at[s], recv_sem.at[s], exp=lax.rem(me + 1, n))
+    down = copy_to(block, held.at[s], down_sem.at[s], recv_sem.at[s], exp=lax.rem(me + n - 1, n))
+    return up, down
+
+
+def experts_kernel(
+    n, x_ref, gates_ref, switch, widen, shrink, out_ref,
+    held, parts, back, total, up_sem, down_sem, recv_sem, ret_sem, back_sem,
+):
+    me = lax.axis_index("exp")
+    greet_all(n, "exp")
+
+    def sends(s, block):
+        return line_sends(n, me, s, block, held, up_sem, down_sem, recv_sem)
+
+    def expert_sum(rows, gates):
+        summed = None
+        for j in range(switch.shape[0]):
+            gate = jnp.dot(rows, switch[j], preferred_element_type=jnp.float32)
+            up = jnp.dot(rows, widen[j], preferred_element_type=jnp.float32)
+            hidden = gate / (1.0 + jnp.exp(-gate)) * up * gates[:, j : j + 1]
+            term = jnp.dot(
+                hidden.astype(jnp.bfloat16), shrink[j], preferred_element_type=jnp.float32
+            )
+            summed = term if summed is None else summed + term
+        return summed
+
+    up, down = sends(me, x_ref)
+    pl.when(me < n - 1)(up.start)
+    pl.when(me > 0)(down.start)
+    total[...] = expert_sum(x_ref[...], gates_ref[me])
+
+    @pl.loop(1, n)
+    def _(k):
+        low, high = me - k, me + k
+
+        @pl.when(low >= 0)
+        def _():
+            up, _ = sends(low, held.at[low])
+            up.wait_recv()
+            pl.when(me < n - 1)(up.start)
+
+        @pl.when(high < n)
+        def _():
+            _, down = sends(high, held.at[high])
+            down.wait_recv()
+            pl.when(me > 0)(down.start)
+
+        @pl.loop(0, 2)
+        def _(side):
+            s = me + (2 * side - 1) * k
+
+            @pl.when((s >= 0) & (s < n))
+            def _():
+                parts[s] = expert_sum(held[s], gates_ref[s]).astype(jnp.bfloat16)
+                copy_to(
+                    parts.at[s], back.at[me], ret_sem.at[s], back_sem.at[me], exp=s
+                ).start()
+
+    @pl.loop(1, n)
+    def _(k):
+        f = lax.rem(me + k, n)
+        copy_to(parts.at[f], back.at[f], ret_sem.at[f], back_sem.at[f], exp=f).wait_recv()
+        total[...] += back[f].astype(jnp.float32)
+
+    out_ref[...] = total[...].astype(out_ref.dtype)
+
+    @pl.loop(1, n)
+    def _(k):
+        f = lax.rem(me + k, n)
+        copy_to(parts.at[f], back.at[f], ret_sem.at[f], back_sem.at[f], exp=f).wait_send()
+
+    @pl.loop(0, n)
+    def _(s):
+        up, down = sends(s, held.at[s])
+        pl.when((s <= me) & (me < n - 1))(up.wait_send)
+        pl.when((s >= me) & (me > 0))(down.wait_send)
+
+
+def run_experts(expert_in, gates, switch, widen, shrink):
+    n = lax.axis_size("exp")
+    rows, width = expert_in.shape
+    vmem = pl.BlockSpec(memory_space=pltpu.VMEM)
+    return pl.pallas_call(
+        functools.partial(experts_kernel, n),
+        out_shape=jax.ShapeDtypeStruct((rows, width), jnp.bfloat16),
+        in_specs=[vmem] * 5,
+        out_specs=vmem,
+        scratch_shapes=[
+            pltpu.VMEM((n, rows, width), jnp.bfloat16),
+            pltpu.VMEM((n, rows, width), jnp.bfloat16),
+            pltpu.VMEM((n, rows, width), jnp.bfloat16),
+            pltpu.VMEM((rows, width), jnp.float32),
+        ]
+        + [pltpu.SemaphoreType.DMA((n,))] * 5,
+        compiler_params=pltpu.CompilerParams(
+            collective_id=2, has_side_effects=True, vmem_limit_bytes=40 * 2**20
+        ),
+    )(expert_in, gates, switch, widen, shrink)
 
 
 def body(
@@ -128,18 +255,13 @@
     local_experts = specialist_switch_tensor.shape[0]
     expert_ids = specialist_slot * local_experts + jnp.arange(local_experts, dtype=jnp.int32)
     gates = gates_of(picked_specialist_labels, specialist_shares, expert_ids)
-    rows = lax.all_gather(expert_in, "exp", axis=0, tiled=True)
-    events, row_count, _ = rows.shape
-    summed = run_experts(
-        rows.reshape(events * row_count, D),
-        gates.reshape(events * row_count, local_experts),
+    expert_update = run_experts(
+        expert_in[0],
+        gates,
         specialist_switch_tensor,
         specialist_widen_tensor,
         specialist_shrink_tensor,
-    ).astype(jnp.bfloat16)
-    expert_update = lax.psum_scatter(
-        summed.reshape(events, row_count, D), "exp", scatter_dimension=0, tiled=True
-    )
+    )[None]
     return (attention_update, expert_update)
 
 

time: 237 us -> 194 us (0.82)
  waiting for transfers between devices: 181 us -> 98.7 us
  Pallas kernels: 0 us -> 55.2 us
  matrix products: 31.5 us -> 12.8 us
  local copies, waits for them, and re-layouts: 2.62 us -> 7.6 us
    pallas_call x0 -> x1, Pallas kernels: none -> 55.2 us  [run_experts(): pl.pallas_call(functools.partial(experts_kernel, n), out_shape=jax.ShapeD...]
    all_gather x3 -> x1, waiting for transfers between devices: 68.8 us -> 22.1 us  [attend_hits(): lax.all_gather(jnp.concatenate([key_heads, value_heads], axis=-1), 'blk',...]
    reduce_scatter x1 -> x0, waiting for transfers between devices: 34.3 us -> none  [body(): lax.psum_scatter(summed.reshape(events, row_count, D), 'exp', scatter_dim...]
    dot_general x2 -> x0, matrix products: 11.6 us -> none  [the longest x1 6.9 us: run_experts(): jnp.einsum('tjf,jfd->td', hidden, shrink, preferred_element_type=jnp.floa...]
    unnamed x25 -> x29, local copies, waits for them, and re-layouts: 0.07 us -> 5.08 us
    dot_general x1, matrix products: 4.44 us -> 1.44 us  [attend_hits(): jnp.einsum('skgij,sjkd->skgid', expo.astype(jnp.bfloat16), value_piece, p...]
    dot_general x1, matrix products: 5.4 us -> 2.98 us  [attend_hits(): jnp.einsum('sikgd,sjkd->skgij', query_heads, key_piece, preferred_element...]
  transfers between devices with their start and end apart: 6 -> 3, of which waited for: 6 -> 3; matrix products, arithmetic and copies ran while one was open for 7% -> 3% of each run, Pallas kernels for 0% -> 0%
where the time goes in v2:
time: 194 us
  waiting for transfers between devices  98.7 us (51%)
  Pallas kernels  55.2 us (28%)
  between operations  14 us (7%)
  matrix products  12.8 us (7%)
  local copies, waits for them, and re-layouts  7.6 us (4%)
  other arithmetic  5.52 us (3%)
    pallas_call x1, Pallas kernels, run_experts(): pl.pallas_call(functools.partial(experts_kernel, n), out_shape=jax.ShapeD...  55.2 us
    all_gather x1, waiting for transfers between devices, body(): lax.all_gather(residual_deposit_sequence, 'exp', axis=0, tiled=True)  41.4 us
    reduce_scatter x1, waiting for transfers between devices, body(): lax.psum_scatter(partial_out.astype(jnp.bfloat16), 'exp', scatter_dimensi...  34.4 us
    all_gather x1, waiting for transfers between devices, attend_hits(): lax.all_gather(jnp.concatenate([key_heads, value_heads], axis=-1), 'blk',...  22.1 us
    unnamed x29, local copies, waits for them, and re-layouts  5.08 us
  transfers between devices with their start and end apart: 3, of which 3 were waited for; matrix products, arithmetic and copies ran while one was open for 3% of the time, Pallas kernels for 0%

profile of v2, /device:TPU:0, one launch (start us, length us, event | category | flops | bytes accessed | tf_op | source)
XLA Modules:
  0.0 193.9 jit_solution(15657036276884176892)
XLA Ops:
  7.2 0.0 copy-start
  7.2 0.0 all-gather.3.cloned.1.call-start
  7.2 0.7 all-gather.3.cloned.1.call-update
  7.9 0.0 copy-start.10
  7.9 0.0 copy-start.11
  7.9 0.0 all-gather.5.cloned.1.call-start
  8.0 41.4 %all-gather.3.cloned.1.call-done = bf16[4,128,1536]{2,1,0:T(8,128)(2,1)} async-done(((bf16[1,128,1536]{2,1,0:T(8,128)(2,1)}), bf16[4,128,1536]{2,1,0:T(8,128)(2,1)}) %all-gather.3.cloned.1.call-update) | async-done | bytes 1572880 | tf_op jit(solution)/shard_map/all_gather | solution.py:235
  49.4 1.9 fusion.1
  51.3 2.2 %multiply_reduce_fusion.2 = (f32[4,128]{1,0:T(4,128)S(1)}, f32[4,128,128]{1,2,0:T(8,128)S(1)}) fusion(bf16[1536,128]{1,0:T(8,128)(2,1)} %param.16, bf16[4,128,1536]{2,1,0:T(8,128)(2,1)} %all-gather.3.cloned.1.call-done, f32[1536]{0:T(1024)} %param.14, f32[4,128]{1,0:T(4,128)S(1)} %add_rsqrt_fusion.3), kind=kOutput, calls=%fused_computation.36 | convolution fusion | flops 204602880 | bytes 2238464 | tf_op jit(solution)/shard_map/std,de->ste/dot_general | solution.py:46
  53.6 0.0 copy-start.12
  53.6 0.0 copy-done.10
  53.6 0.0 copy-done.11
  53.7 0.0 copy-done.5
  53.7 0.7 fusion.11
  54.4 0.7 pad_maximum_fusion
  55.1 0.0 all-gather.5.cloned.1.call-update
  55.2 0.0 reduce-scatter.2.cloned.1.call-start
  55.2 0.0 copy-done.12
  55.2 0.1 dynamic-slice_multiply_fusion
  55.3 3.2 %fusion.26 = (f32[4,128,384]{2,1,0:T(8,128)}, f32[4,128,384]{2,1,0:T(8,128)S(1)}) fusion(bf16[1536,384]{1,0:T(8,128)(2,1)} %param.15, bf16[4,128,1536]{2,1,0:T(8,128)(2,1)S(1)} %copy-done.5, f32[1536]{0:T(1024)S(1)} %copy-done.11, f32[4,128]{1,0:T(4,128)S(1)} %add_rsqrt_fusion.3), kind=kOutput, calls=%fused_computation.46 | convolution fusion | flops 607322112 | bytes 4333568 | tf_op jit(solution)/shard_map/std,de->ste/dot_general | solution.py:40
  58.5 1.4 copy.46
  59.9 0.3 copy.45
  60.2 0.1 reduce_sum.65
  60.2 22.1 %all-gather.5.cloned.1.call-done = bf16[4,1024,1,256]{1,3,0,2:T(8,128)(2,1)} async-done(((bf16[4,128,1,256]{1,3,0,2:T(8,128)(2,1)}), bf16[4,1024,1,256]{1,3,0,2:T(8,128)(2,1)}) %all-gather.5.cloned.1.call-update) | async-done | bytes 2097168 | tf_op jit(solution)/shard_map/all_gather | solution.py:61
  82.4 3.0 %bitcast_reduce_fusion = (f32[4,3,128]{2,1,0:T(4,128)S(1)}, f32[4,1024,128,3]{2,1,3,0:T(8,128)S(1)}) fusion(f32[3]{0:T(128)S(1)} %dynamic-slice_multiply_fusion, f32[4,128,3,128]{1,3,2,0:T(8,128)S(1)} %bitcast.84, f32[4,128,3]{1,2,0:T(4,128)S(1)} %add_rsqrt_fusion.1, bf16[4,1024,1,256]{1,3,0,2:T(8,128)(2,1)} %all-gather.5.cloned.1.call-done), kind=kOutput, calls=%fused_computation | convolution fusion | flops 406190592 | bytes 8138764 | tf_op jit(solution)/shard_map/sikgd,sjkd->skgij/dot_general | solution.py:65
  85.4 0.0 copy-done.6
  85.4 1.4 multiply_reduce_fusion.1
  86.8 0.0 copy-done
  86.8 0.0 copy-start.8
  86.8 0.0 copy-start.9
  86.9 0.0 copy-start.7
  86.9 2.2 %fusion.8 = bf16[4,128,1536]{2,1,0:T(8,128)(2,1)} fusion(bf16[3,128,1536,1]{2,1,0,3:T(8,128)(2,1)S(1)} %bitcast.82, f32[4,3,128,128]{2,3,1,0:T(8,128)S(1)} %get-tuple-element.9, f32[4,3,128]{2,1,0:T(4,128)S(1)} %add_rsqrt_fusion), kind=kOutput, calls=%fused_computation.13 | convolution fusion | flops 605159424 | bytes 3545088 | tf_op jit(solution)/shard_map/skgid,kgde->sie/dot_general | solution.py:81
  89.1 0.0 reduce-scatter.2.cloned.1.call-update
  89.1 0.0 copy-done.8
  89.1 0.0 copy-done.9
  89.1 0.1 select_reduce_fusion
  89.2 0.9 copy.53.gates_ref
  90.1 34.4 %reduce-scatter.2.cloned.1.call-done = bf16[1,128,1536]{2,1,0:T(8,128)(2,1)} async-done(((bf16[4,128,1536]{2,1,0:T(8,128)(2,1)}), bf16[1,128,1536]{2,1,0:T(8,128)(2,1)}) %reduce-scatter.2.cloned.1.call-update) | async-done | bytes 393232 | tf_op jit(solution)/shard_map/reduce_scatter | solution.py:249
  124.5 1.3 multiply_reduce_fusion
  125.9 0.0 copy-done.7
  125.9 1.3 fusion.20.x_ref
  127.2 0.0 copy-done.1
  127.2 0.0 copy-start.2
  127.2 1.7 copy-done.2
  128.8 1.7 copy-done.3
  130.5 0.9 copy-done.4
  131.4 55.2 %shard_map.140 = bf16[128,1536]{1,0:T(8,128)(2,1)S(1)} custom-call(bf16[128,1536]{1,0:T(8,128)(2,1)S(1)} %fusion.20.x_ref, f32[4,128,2]{2,1,0:T(8,128)S(1)} %copy-done.4, bf16[2,1536,384]{2,1,0:T(8,128)(2,1)S(1)} %copy-done.1, bf16[2,1536,384]{2,1,0:T(8,128)(2,1)S(1)} %copy-done.2, bf16[2,384,1536]{2,1,0:T(8,128)(2,1)S(1)} %copy-done.3), custom_call_target="tpu_custom_call" | custom-call | tf_op jit(solution)/shard_map/pallas_call | solution.py:200
  186.7 0.7 copy.67
  (14 shorter events, 0.1 us)
Async XLA Ops:
  7.2 79.7 %copy-start = (bf16[384,1536]{1,0:T(8,128)(2,1)S(1)}, bf16[384,1536]{1,0:T(8,128)(2,1)}, u32[]{:S(2)}) copy-start(bf16[384,1536]{1,0:T(8,128)(2,1)} %param.18) | copy-start | bytes 3538948
  7.2 42.2 %all-gather.3.cloned.1.call-start = ((), (), s32[]{:S(2)}) async-start(), calls=%async_computation.1 | async-start | bytes 1966080 | tf_op jit(solution)/shard_map/all_gather | solution.py:235
  7.9 45.7 %copy-start.10 = (bf16[1536,128]{1,0:T(8,128)(2,1)S(1)}, bf16[1536,128]{1,0:T(8,128)(2,1)}, u32[]{:S(2)}) copy-start(bf16[1536,128]{1,0:T(8,128)(2,1)} %param.17) | copy-start | bytes 1179652
  7.9 45.7 %copy-start.11 = (f32[1536]{0:T(1024)S(1)}, f32[1536]{0:T(1024)}, u32[]{:S(2)}) copy-start(f32[1536]{0:T(1024)} %param.14) | copy-start | bytes 18436
  7.9 74.4 %all-gather.5.cloned.1.call-start = ((), (), s32[]{:S(2)}) async-start(), calls=%async_computation.2 | async-start | bytes 2359296 | tf_op jit(solution)/shard_map/all_gather | solution.py:61
  49.4 4.2 %copy-start.5 = (bf16[4,128,1536]{2,1,0:T(8,128)(2,1)S(1)}, bf16[4,128,1536]{2,1,0:T(8,128)(2,1)}, u32[]{:S(2)}) copy-start(bf16[4,128,1536]{2,1,0:T(8,128)(2,1)} %all-gather.3.cloned.1.call-done) | copy-start | bytes 4718596
  53.6 1.6 copy-start.12
  55.2 69.4 %reduce-scatter.2.cloned.1.call-start = ((), (), s32[]{:S(2)}) async-start(), calls=%async_computation.3 | async-start | bytes 1966080 | tf_op jit(solution)/shard_map/reduce_scatter | solution.py:249
  82.4 3.0 %copy-start.6 = (bf16[4,1024,1,256]{1,3,0,2:T(8,128)(2,1)S(1)}, bf16[4,1024,1,256]{1,3,0,2:T(8,128)(2,1)}, u32[]{:S(2)}) copy-start(bf16[4,1024,1,256]{1,3,0,2:T(8,128)(2,1)} %all-gather.5.cloned.1.call-done) | copy-start | bytes 6291460
  86.8 2.3 %copy-start.8 = (s32[4,128,2]{1,2,0:T(2,128)S(1)}, s32[4,128,2]{1,2,0:T(2,128)}, u32[]{:S(2)}) copy-start(s32[4,128,2]{1,2,0:T(2,128)} %param.24) | copy-start | bytes 12292
  86.8 2.3 %copy-start.9 = (f32[4,128,2]{1,2,0:T(2,128)S(1)}, f32[4,128,2]{1,2,0:T(2,128)}, u32[]{:S(2)}) copy-start(f32[4,128,2]{1,2,0:T(2,128)} %param.25) | copy-start | bytes 12292
  86.9 39.0 %copy-start.7 = (f32[1536]{0:T(1024)S(1)}, f32[1536]{0:T(1024)}, u32[]{:S(2)}) copy-start(f32[1536]{0:T(1024)} %param.20) | copy-start | bytes 18436
  89.1 38.1 %copy-start.1 = (bf16[2,1536,384]{2,1,0:T(8,128)(2,1)S(1)}, bf16[2,1536,384]{2,1,0:T(8,128)(2,1)}, u32[]{:S(2)}) copy-start(bf16[2,1536,384]{2,1,0:T(8,128)(2,1)} %switch.1) | copy-start | bytes 7077892
  127.2 1.7 copy-start.2
  128.8 1.7 copy-start.3
  130.5 0.9 copy-start.4
Sparse Core Ops, SparseCore 0:
  9.6 39.7 all-gather.2
  55.3 27.0 all-gather.4
  89.2 35.2 reduce-scatter.1

commit v3 on v2

--- a/solution.py
+++ b/solution.py
@@ -25,60 +25,22 @@
     return values * lax.rsqrt(jnp.mean(values * values, axis=-1, keepdims=True) + 1e-06)
 
 
-def attend_hits(
-    rescaled_entries,
-    asking_projector,
-    lookup_projector,
-    content_projector,
-    final_projector,
-    logit_multipliers,
-):
-    events, row_count, model_width = rescaled_entries.shape
-    common_key_heads = lookup_projector.shape[1] // PER_LANE_DIM
-    local_lane_count = asking_projector.shape[1] // PER_LANE_DIM
-    askers_per_lookup = local_lane_count // common_key_heads
-    query_heads = jnp.einsum(
-        "std,de->ste", rescaled_entries, asking_projector, preferred_element_type=jnp.float32
-    )
-    query_heads = head_norm(
-        query_heads.reshape(events, row_count, common_key_heads, askers_per_lookup, PER_LANE_DIM)
-    ).astype(jnp.bfloat16)
-    key_heads = jnp.einsum(
-        "std,de->ste", rescaled_entries, lookup_projector, preferred_element_type=jnp.float32
-    )
-    key_heads = head_norm(
-        key_heads.reshape(events, row_count, common_key_heads, PER_LANE_DIM)
-    ).astype(jnp.bfloat16)
-    value_heads = jnp.einsum(
-        "std,de->ste", rescaled_entries, content_projector, preferred_element_type=jnp.float32
-    )
-    value_heads = value_heads.reshape(events, row_count, common_key_heads, PER_LANE_DIM).astype(
-        jnp.bfloat16
-    )
-    inverse_root_dim = (logit_multipliers / math.sqrt(PER_LANE_DIM)).reshape(
-        common_key_heads, askers_per_lookup
-    )
-    pair = lax.all_gather(
-        jnp.concatenate([key_heads, value_heads], axis=-1), "blk", axis=1, tiled=True
-    )
-    key_piece, value_piece = pair[..., :PER_LANE_DIM], pair[..., PER_LANE_DIM:]
-    scores = jnp.einsum(
-        "sikgd,sjkd->skgij", query_heads, key_piece, preferred_element_type=jnp.float32
-    )
-    expo = jnp.exp(scores * inverse_root_dim[None, :, :, None, None])
+def attend_hits(query_heads, pairs, final_projector, logit_multipliers):
+    events, row_count, _ = query_heads.shape
+    lanes = logit_multipliers.shape[0]
+    query_heads = query_heads.reshape(events, row_count, lanes, PER_LANE_DIM)
+    pairs = jnp.swapaxes(pairs, 0, 1).reshape(events, -1, 2 * PER_LANE_DIM)
+    keys, values = pairs[..., :PER_LANE_DIM], pairs[..., PER_LANE_DIM:]
+    scale = logit_multipliers / math.sqrt(PER_LANE_DIM)
+    scores = jnp.einsum("sigd,sjd->sgij", query_heads, keys, preferred_element_type=jnp.float32)
+    expo = jnp.exp(scores * scale[None, :, None, None])
     totals = jnp.sum(expo, axis=-1)
     mixture = jnp.einsum(
-        "skgij,sjkd->skgid",
-        expo.astype(jnp.bfloat16),
-        value_piece,
-        preferred_element_type=jnp.float32,
-    )
-    totals, mixture = (totals, mixture)
+        "sgij,sjd->sgid", expo.astype(jnp.bfloat16), values, preferred_element_type=jnp.float32
+    )
     heads_out = head_norm(mixture / totals[..., None]).astype(jnp.bfloat16)
-    out_blocks = final_projector.reshape(
-        common_key_heads, askers_per_lookup, PER_LANE_DIM, model_width
-    )
-    return jnp.einsum("skgid,kgde->sie", heads_out, out_blocks, preferred_element_type=jnp.float32)
+    out_blocks = final_projector.reshape(lanes, PER_LANE_DIM, final_projector.shape[1])
+    return jnp.einsum("sgid,gde->sie", heads_out, out_blocks, preferred_element_type=jnp.float32)
 
 
 def gates_of(labels, shares, expert_ids):
@@ -117,6 +79,124 @@
     up = copy_to(block, held.at[s], up_sem.at[s], recv_sem.at[s], exp=lax.rem(me + 1, n))
     down = copy_to(block, held.at[s], down_sem.at[s], recv_sem.at[s], exp=lax.rem(me + n - 1, n))
     return up, down
+
+
+def greet_both(n, blk_count):
+    me, here = lax.axis_index("exp"), lax.axis_index("blk")
+    barrier = pltpu.get_barrier_semaphore()
+
+    @pl.loop(1, n)
+    def _(k):
+        pl.semaphore_signal(
+            barrier,
+            inc=1,
+            device_id={"exp": lax.rem(me + k, n)},
+            device_id_type=pl.DeviceIdType.MESH,
+        )
+
+    @pl.loop(1, blk_count)
+    def _(k):
+        pl.semaphore_signal(
+            barrier,
+            inc=1,
+            device_id={"blk": lax.rem(here + k, blk_count)},
+            device_id_type=pl.DeviceIdType.MESH,
+        )
+
+    pl.semaphore_wait(barrier, n + blk_count - 2)
+
+
+def project_kernel(
+    n, blk_count, x_ref, gain, asking, lookup, content, q_ref, kv_ref,
+    held, up_sem, down_sem, recv_sem, kv_send_sem, kv_recv_sem,
+):
+    me, here = lax.axis_index("exp"), lax.axis_index("blk")
+    greet_both(n, blk_count)
+
+    def sends(s, block):
+        return line_sends(n, me, s, block, held, up_sem, down_sem, recv_sem)
+
+    def kv_copy(s, owner, peer):
+        block = kv_ref.at[owner, s]
+        return copy_to(block, block, kv_send_sem.at[s, peer], kv_recv_sem.at[s, owner], blk=peer)
+
+    def project(s, block):
+        rows = norm_rows(block, gain[...]).astype(jnp.bfloat16)
+        keys = jnp.dot(rows, lookup[...], preferred_element_type=jnp.float32)
+        kv_ref[here, s, :, :PER_LANE_DIM] = head_norm(keys).astype(jnp.bfloat16)
+        values = jnp.dot(rows, content[...], preferred_element_type=jnp.float32)
+        kv_ref[here, s, :, PER_LANE_DIM:] = values.astype(jnp.bfloat16)
+
+        @pl.loop(1, blk_count)
+        def _(k):
+            kv_copy(s, here, lax.rem(here + k, blk_count)).start()
+
+        queries = jnp.dot(rows, asking[...], preferred_element_type=jnp.float32)
+        for h in range(asking.shape[1] // PER_LANE_DIM):
+            lane = slice(h * PER_LANE_DIM, (h + 1) * PER_LANE_DIM)
+            q_ref[s, :, lane] = head_norm(queries[:, lane]).astype(jnp.bfloat16)
+
+    up, down = sends(me, x_ref)
+    pl.when(me < n - 1)(up.start)
+    pl.when(me > 0)(down.start)
+    project(me, x_ref[...])
+
+    @pl.loop(1, n)
+    def _(k):
+        low, high = me - k, me + k
+
+        @pl.when(low >= 0)
+        def _():
+            up, _ = sends(low, held.at[low])
+            up.wait_recv()
+            pl.when(me < n - 1)(up.start)
+
+        @pl.when(high < n)
+        def _():
+            _, down = sends(high, held.at[high])
+            down.wait_recv()
+            pl.when(me > 0)(down.start)
+
+        @pl.loop(0, 2)
+        def _(side):
+            s = me + (2 * side - 1) * k
+
+            @pl.when((s >= 0) & (s < n))
+            def _():
+                project(s, held[s])
+
+    @pl.loop(0, n)
+    def _(s):
+        up, down = sends(s, held.at[s])
+        pl.when((s <= me) & (me < n - 1))(up.wait_send)
+        pl.when((s >= me) & (me > 0))(down.wait_send)
+
+        @pl.loop(1, blk_count)
+        def _(k):
+            peer = lax.rem(here + k, blk_count)
+            kv_copy(s, here, peer).wait_send()
+            kv_copy(s, peer, peer).wait_recv()
+
+
+def project_hits(rows, gain, asking, lookup, content):
+    n, blk_count = lax.axis_size("exp"), lax.axis_size("blk")
+    count, width = rows.shape
+    vmem = pl.BlockSpec(memory_space=pltpu.VMEM)
+    return pl.pallas_call(
+        functools.partial(project_kernel, n, blk_count),
+        out_shape=(
+            jax.ShapeDtypeStruct((n, count, asking.shape[1]), jnp.bfloat16),
+            jax.ShapeDtypeStruct((blk_count, n, count, 2 * PER_LANE_DIM), jnp.bfloat16),
+        ),
+        in_specs=[vmem] * 5,
+        out_specs=(vmem, vmem),
+        scratch_shapes=[pltpu.VMEM((n, count, width), jnp.bfloat16)]
+        + [pltpu.SemaphoreType.DMA((n,))] * 3
+        + [pltpu.SemaphoreType.DMA((n, blk_count))] * 2,
+        compiler_params=pltpu.CompilerParams(
+            collective_id=1, has_side_effects=True, vmem_limit_bytes=40 * 2**20
+        ),
+    )(rows, gain[None], asking, lookup, content)
 
 
 def experts_kernel(
@@ -232,17 +312,20 @@
 ):
     specialist_slot = lax.axis_index("exp")
     exp_count = lax.axis_size("exp")
-    rows_all = lax.all_gather(residual_deposit_sequence, "exp", axis=0, tiled=True)
-    rescaled_entries = norm_rows(rows_all, premix_rescaler).astype(jnp.bfloat16)
+    query_heads, pairs = project_hits(
+        residual_deposit_sequence[0],
+        premix_rescaler,
+        asking_projector,
+        lookup_projector,
+        content_projector,
+    )
     local_lane_count = asking_projector.shape[1] // PER_LANE_DIM
     device_scratch = lax.dynamic_slice_in_dim(
         logit_multipliers, specialist_slot * local_lane_count, local_lane_count
     )
     partial_out = attend_hits(
-        rescaled_entries,
-        asking_projector,
-        lookup_projector,
-        content_projector,
+        query_heads,
+        pairs,
         final_projector,
         device_scratch,
     )

time: 194 us -> 166 us (0.86)
  waiting for transfers between devices: 98.7 us -> 33.5 us
  Pallas kernels: 55.2 us -> 96.5 us
  matrix products: 12.8 us -> 5.85 us
  local copies, waits for them, and re-layouts: 7.6 us -> 12.8 us
  other arithmetic: 5.52 us -> 2.55 us
    all_gather x2 -> x0, waiting for transfers between devices: 63.6 us -> none  [the longest x1 41.4 us: body(): lax.all_gather(residual_deposit_sequence, 'exp', axis=0, tiled=True)]
    pallas_call x0 -> x1, Pallas kernels: none -> 41.2 us  [project_hits(): pl.pallas_call(functools.partial(project_kernel, n, blk_count), out_shape...]
    dot_general x6 -> x3, matrix products: 12.8 us -> 5.85 us  [the longest x1 2.37 us: attend_hits(): jnp.einsum('sigd,sjd->sgij', query_heads, keys, preferred_element_type=jn...]
    unnamed x29 -> x31, local copies, waits for them, and re-layouts: 5.08 us -> 10 us
    reduce_sum x2 -> x1, other arithmetic: 3.23 us -> 1.21 us  [norm_rows(): jnp.mean(widened * widened, axis=-1, keepdims=True) + 1e-05]
  transfers between devices with their start and end apart: 3 -> 1, of which waited for: 3 -> 1; matrix products, arithmetic and copies ran while one was open for 3% -> 0% of each run, Pallas kernels for 0% -> 0%
where the time goes in v3:
time: 166 us; the launch traced here: 165 us
  Pallas kernels  96.5 us (58%)
  waiting for transfers between devices  33.5 us (20%)
  between operations  14.2 us (9%)
  local copies, waits for them, and re-layouts  12.8 us (8%)
  matrix products  5.85 us (4%)
  other arithmetic  2.55 us (2%)
    pallas_call x1, Pallas kernels, run_experts(): pl.pallas_call(functools.partial(experts_kernel, n), out_shape=jax.ShapeD...  55.3 us
    pallas_call x1, Pallas kernels, project_hits(): pl.pallas_call(functools.partial(project_kernel, n, blk_count), out_shape...  41.2 us
    reduce_scatter x1, waiting for transfers between devices, body(): lax.psum_scatter(partial_out.astype(jnp.bfloat16), 'exp', scatter_dimensi...  33.4 us
    unnamed x31, local copies, waits for them, and re-layouts  10 us
  transfers between devices with their start and end apart: 1, of which 1 were waited for; matrix products, arithmetic and copies ran while one was open for 0% of the time, Pallas kernels for 0%

profile of v3, /device:TPU:0, one launch (start us, length us, event | category | flops | bytes accessed | tf_op | source)
XLA Modules:
  0.0 165.3 jit_solution(10585913585761905571)
XLA Ops:
  7.2 0.0 copy-start
  7.2 0.0 reduce-scatter.2.cloned.1.call-start
  7.2 0.8 broadcast_in_dim.16.gain
  8.0 0.0 copy-start.1
  8.0 1.0 copy-done.1
  9.0 0.0 copy-start.6
  9.0 1.3 copy-done.6
  10.3 0.0 copy-start.7
  10.3 1.0 copy-done.7
  11.3 0.0 copy-start.8
  11.3 1.0 copy-done.8
  12.3 41.2 %shard_map.140 = (bf16[4,128,384]{2,1,0:T(8,128)(2,1)S(1)}, bf16[8,4,128,256]{3,2,1,0:T(8,128)(2,1)S(1)}) custom-call(bf16[128,1536]{1,0:T(8,128)(2,1)S(1)} %bitcast.43, f32[1,1536]{1,0:T(1,128)S(1)} %broadcast_in_dim.16.gain, bf16[1536,384]{1,0:T(8,128)(2,1)S(1)} %copy-done.6, bf16[1536,128]{1,0:T(8,128)(2,1)S(1)} %copy-done.7, bf16[1536,128]{1,0:T(8,128)(2,1)S(1)} %copy-done.8), custom_call_target="tpu_custom_call" | custom-call | tf_op jit(solution)/shard_map/pallas_call | solution.py:185
  53.5 0.0 copy-start.13
  53.5 1.6 copy.29
  55.1 0.2 copy.30
  55.3 0.0 copy-done.13
  55.3 0.1 dynamic-slice_multiply_fusion
  55.4 0.0 copy-start.9
  55.4 2.4 %bitcast_reduce_fusion = (f32[4,3,128]{2,1,0:T(4,128)S(1)}, f32[4,1024,128,3]{2,1,3,0:T(8,128)S(1)}) fusion(f32[3]{0:T(128)S(1)} %dynamic-slice_multiply_fusion, bf16[4,128,3,128]{1,3,2,0:T(8,128)(2,1)S(1)} %bitcast.48, bf16[4,1024,256]{2,1,0:T(8,128)(2,1)} %bitcast.46), kind=kOutput, calls=%fused_computation | convolution fusion | flops 405797376 | bytes 7739404 | tf_op jit(solution)/shard_map/sigd,sjd->sgij/dot_general | solution.py:35
  57.8 0.0 copy-done.9
  57.8 1.3 multiply_reduce_fusion.1
  59.1 0.0 copy-done
  59.1 0.0 copy-start.11
  59.1 0.0 copy-start.12
  59.1 0.0 copy-start.2
  59.1 0.0 copy-start.10
  59.2 2.2 %fusion.2 = bf16[4,128,1536]{2,1,0:T(8,128)(2,1)} fusion(bf16[3,128,1536,1]{2,1,0,3:T(8,128)(2,1)S(1)} %bitcast.42, f32[4,3,128,128]{2,3,1,0:T(8,128)S(1)} %get-tuple-element.9, f32[4,3,128]{2,1,0:T(4,128)S(1)} %add_rsqrt_fusion), kind=kOutput, calls=%fused_computation.6 | convolution fusion | flops 605159424 | bytes 3545088 | tf_op jit(solution)/shard_map/sgid,gde->sie/dot_general | solution.py:43
  61.3 0.0 reduce-scatter.2.cloned.1.call-update
  61.4 0.0 copy-done.11
  61.4 0.0 copy-done.12
  61.4 0.1 select_reduce_fusion
  61.5 0.1 copy.37.gates_ref
  61.6 33.4 %reduce-scatter.2.cloned.1.call-done = bf16[1,128,1536]{2,1,0:T(8,128)(2,1)} async-done(((bf16[4,128,1536]{2,1,0:T(8,128)(2,1)}), bf16[1,128,1536]{2,1,0:T(8,128)(2,1)}) %reduce-scatter.2.cloned.1.call-update) | async-done | bytes 393232 | tf_op jit(solution)/shard_map/reduce_scatter | solution.py:332
  95.1 0.0 copy-done.2
  95.1 1.2 multiply_reduce_fusion
  96.3 0.0 copy-done.10
  96.3 1.2 fusion.5.x_ref
  97.5 0.0 copy-start.3
  97.5 1.7 %copy-done.3 = bf16[2,1536,384]{2,1,0:T(8,128)(2,1)S(1)} copy-done((bf16[2,1536,384]{2,1,0:T(8,128)(2,1)S(1)}, bf16[2,1536,384]{2,1,0:T(8,128)(2,1)}, u32[]{:S(2)}) %copy-start.3) | copy-done | bytes 2359320
  99.1 0.0 copy-start.4
  99.1 1.7 %copy-done.4 = bf16[2,1536,384]{2,1,0:T(8,128)(2,1)S(1)} copy-done((bf16[2,1536,384]{2,1,0:T(8,128)(2,1)S(1)}, bf16[2,1536,384]{2,1,0:T(8,128)(2,1)}, u32[]{:S(2)}) %copy-start.4) | copy-done | bytes 2359320
  100.8 0.0 copy-start.5
  100.8 1.7 %copy-done.5 = bf16[2,384,1536]{2,1,0:T(8,128)(2,1)S(1)} copy-done((bf16[2,384,1536]{2,1,0:T(8,128)(2,1)S(1)}, bf16[2,384,1536]{2,1,0:T(8,128)(2,1)}, u32[]{:S(2)}) %copy-start.5) | copy-done | bytes 2359320
  102.5 55.3 %shard_map.141 = bf16[128,1536]{1,0:T(8,128)(2,1)S(1)} custom-call(bf16[128,1536]{1,0:T(8,128)(2,1)S(1)} %fusion.5.x_ref, f32[4,128,2]{2,1,0:T(8,128)S(1)} %copy.37.gates_ref, bf16[2,1536,384]{2,1,0:T(8,128)(2,1)S(1)} %copy-done.3, bf16[2,1536,384]{2,1,0:T(8,128)(2,1)S(1)} %copy-done.4, bf16[2,384,1536]{2,1,0:T(8,128)(2,1)S(1)} %copy-done.5), custom_call_target="tpu_custom_call" | custom-call | tf_op jit(solution)/shard_map/pallas_call | solution.py:280
  157.7 0.7 copy.46
  (5 shorter events, 0.0 us)
Async XLA Ops:
  7.2 51.9 %copy-start = (bf16[384,1536]{1,0:T(8,128)(2,1)S(1)}, bf16[384,1536]{1,0:T(8,128)(2,1)}, u32[]{:S(2)}) copy-start(bf16[384,1536]{1,0:T(8,128)(2,1)} %param.18) | copy-start | bytes 3538948
  7.2 87.9 %reduce-scatter.2.cloned.1.call-start = ((), (), s32[]{:S(2)}) async-start(), calls=%async_computation.1 | async-start | bytes 1966080 | tf_op jit(solution)/shard_map/reduce_scatter | solution.py:332
  8.0 1.0 copy-start.1
  9.0 1.3 copy-start.6
  10.3 1.0 copy-start.7
  11.3 1.0 copy-start.8
  53.5 1.8 %copy-start.13 = (f32[12]{0:T(128)S(1)}, f32[12]{0:T(128)}, u32[]{:S(2)}) copy-start(f32[12]{0:T(128)} %param.19) | copy-start | bytes 148
  55.4 2.4 %copy-start.9 = (bf16[4,8,128,256]{3,2,1,0:T(8,128)(2,1)S(1)}, bf16[4,8,128,256]{3,2,1,0:T(8,128)(2,1)}, u32[]{:S(2)}) copy-start(bf16[4,8,128,256]{3,2,1,0:T(8,128)(2,1)} %copy.29) | copy-start | bytes 6291460
  59.1 2.3 %copy-start.11 = (s32[4,128,2]{1,2,0:T(2,128)S(1)}, s32[4,128,2]{1,2,0:T(2,128)}, u32[]{:S(2)}) copy-start(s32[4,128,2]{1,2,0:T(2,128)} %param.24) | copy-start | bytes 12292
  59.1 2.3 %copy-start.12 = (f32[4,128,2]{1,2,0:T(2,128)S(1)}, f32[4,128,2]{1,2,0:T(2,128)}, u32[]{:S(2)}) copy-start(f32[4,128,2]{1,2,0:T(2,128)} %param.25) | copy-start | bytes 12292
  59.1 36.0 %copy-start.2 = (bf16[1,128,1536]{2,1,0:T(8,128)(2,1)S(1)}, bf16[1,128,1536]{2,1,0:T(8,128)(2,1)}, u32[]{:S(2)}) copy-start(bf16[1,128,1536]{2,1,0:T(8,128)(2,1)} %param.13) | copy-start | bytes 1179652
  59.1 37.2 %copy-start.10 = (f32[1536]{0:T(1024)S(1)}, f32[1536]{0:T(1024)}, u32[]{:S(2)}) copy-start(f32[1536]{0:T(1024)} %param.20) | copy-start | bytes 18436
  97.5 1.7 %copy-start.3 = (bf16[2,1536,384]{2,1,0:T(8,128)(2,1)S(1)}, bf16[2,1536,384]{2,1,0:T(8,128)(2,1)}, u32[]{:S(2)}) copy-start(bf16[2,1536,384]{2,1,0:T(8,128)(2,1)} %switch.1) | copy-start | bytes 7077892
  99.1 1.7 %copy-start.4 = (bf16[2,1536,384]{2,1,0:T(8,128)(2,1)S(1)}, bf16[2,1536,384]{2,1,0:T(8,128)(2,1)}, u32[]{:S(2)}) copy-start(bf16[2,1536,384]{2,1,0:T(8,128)(2,1)} %widen.1) | copy-start | bytes 7077892
  100.8 1.7 %copy-start.5 = (bf16[2,384,1536]{2,1,0:T(8,128)(2,1)S(1)}, bf16[2,384,1536]{2,1,0:T(8,128)(2,1)}, u32[]{:S(2)}) copy-start(bf16[2,384,1536]{2,1,0:T(8,128)(2,1)} %shrink.1) | copy-start | bytes 7077892
Sparse Core Ops, SparseCore 0:
  61.5 33.5 reduce-scatter.1

commit v4 on v3

--- a/solution.py
+++ b/solution.py
@@ -81,6 +81,13 @@
     return up, down
 
 
+def loads(pairs, load_sem):
+    return [
+        pltpu.make_async_copy(source, slot, load_sem.at[i])
+        for i, (source, slot) in enumerate(pairs)
+    ]
+
+
 def greet_both(n, blk_count):
     me, here = lax.axis_index("exp"), lax.axis_index("blk")
     barrier = pltpu.get_barrier_semaphore()
@@ -107,10 +114,15 @@
 
 
 def project_kernel(
-    n, blk_count, x_ref, gain, asking, lookup, content, q_ref, kv_ref,
-    held, up_sem, down_sem, recv_sem, kv_send_sem, kv_recv_sem,
+    n, blk_count, x_ref, gain, asking_in, lookup_in, content_in, q_ref, kv_ref,
+    asking, lookup, content, load_sem, held, up_sem, down_sem, recv_sem, kv_send_sem, kv_recv_sem,
 ):
     me, here = lax.axis_index("exp"), lax.axis_index("blk")
+    weights = loads(
+        ((lookup_in, lookup), (content_in, content), (asking_in, asking)), load_sem
+    )
+    for copy in weights:
+        copy.start()
     greet_both(n, blk_count)
 
     def sends(s, block):
@@ -139,6 +151,8 @@
     up, down = sends(me, x_ref)
     pl.when(me < n - 1)(up.start)
     pl.when(me > 0)(down.start)
+    for copy in weights:
+        copy.wait()
     project(me, x_ref[...])
 
     @pl.loop(1, n)
@@ -188,22 +202,26 @@
             jax.ShapeDtypeStruct((n, count, asking.shape[1]), jnp.bfloat16),
             jax.ShapeDtypeStruct((blk_count, n, count, 2 * PER_LANE_DIM), jnp.bfloat16),
         ),
-        in_specs=[vmem] * 5,
+        in_specs=[vmem] * 2 + [pl.BlockSpec(memory_space=pl.ANY)] * 3,
         out_specs=(vmem, vmem),
-        scratch_shapes=[pltpu.VMEM((n, count, width), jnp.bfloat16)]
+        scratch_shapes=[pltpu.VMEM(t.shape, t.dtype) for t in (asking, lookup, content)]
+        + [pltpu.SemaphoreType.DMA((3,)), pltpu.VMEM((n, count, width), jnp.bfloat16)]
         + [pltpu.SemaphoreType.DMA((n,))] * 3
         + [pltpu.SemaphoreType.DMA((n, blk_count))] * 2,
         compiler_params=pltpu.CompilerParams(
-            collective_id=1, has_side_effects=True, vmem_limit_bytes=40 * 2**20
+            collective_id=1, has_side_effects=True, vmem_limit_bytes=56 * 2**20
         ),
     )(rows, gain[None], asking, lookup, content)
 
 
 def experts_kernel(
-    n, x_ref, gates_ref, switch, widen, shrink, out_ref,
-    held, parts, back, total, up_sem, down_sem, recv_sem, ret_sem, back_sem,
+    n, x_ref, gates_ref, switch_in, widen_in, shrink_in, out_ref,
+    switch, widen, shrink, load_sem, held, parts, back, total, up_sem, down_sem, recv_sem, ret_sem, back_sem,
 ):
     me = lax.axis_index("exp")
+    weights = loads(((switch_in, switch), (widen_in, widen), (shrink_in, shrink)), load_sem)
+    for copy in weights:
+        copy.start()
     greet_all(n, "exp")
 
     def sends(s, block):
@@ -224,6 +242,8 @@
     up, down = sends(me, x_ref)
     pl.when(me < n - 1)(up.start)
     pl.when(me > 0)(down.start)
+    for copy in weights:
+        copy.wait()
     total[...] = expert_sum(x_ref[...], gates_ref[me])
 
     @pl.loop(1, n)
@@ -280,9 +300,11 @@
     return pl.pallas_call(
         functools.partial(experts_kernel, n),
         out_shape=jax.ShapeDtypeStruct((rows, width), jnp.bfloat16),
-        in_specs=[vmem] * 5,
+        in_specs=[vmem] * 2 + [pl.BlockSpec(memory_space=pl.ANY)] * 3,
         out_specs=vmem,
-        scratch_shapes=[
+        scratch_shapes=[pltpu.VMEM(t.shape, t.dtype) for t in (switch, widen, shrink)]
+        + [
+            pltpu.SemaphoreType.DMA((3,)),
             pltpu.VMEM((n, rows, width), jnp.bfloat16),
             pltpu.VMEM((n, rows, width), jnp.bfloat16),
             pltpu.VMEM((n, rows, width), jnp.bfloat16),
@@ -290,7 +312,7 @@
         ]
         + [pltpu.SemaphoreType.DMA((n,))] * 5,
         compiler_params=pltpu.CompilerParams(
-            collective_id=2, has_side_effects=True, vmem_limit_bytes=40 * 2**20
+            collective_id=2, has_side_effects=True, vmem_limit_bytes=56 * 2**20
         ),
     )(expert_in, gates, switch, widen, shrink)
 

time: 166 us -> 165 us (level)
  local copies, waits for them, and re-layouts: 12.8 us -> 7.7 us
  Pallas kernels: 96.5 us -> 101 us
    unnamed x31 -> x15, local copies, waits for them, and re-layouts: 10 us -> 1.81 us
    pallas_call x1, Pallas kernels: 41.2 us -> 43.7 us  [project_hits(): pl.pallas_call(functools.partial(project_kernel, n, blk_count), out_shape...]
    pallas_call x1, Pallas kernels: 55.3 us -> 57.1 us  [run_experts(): pl.pallas_call(functools.partial(experts_kernel, n), out_shape=jax.ShapeD...]
    pallas_call x1, local copies, waits for them, and re-layouts: 0.22 us -> 1.91 us  [project_hits(): pl.pallas_call(functools.partial(project_kernel, n, blk_count), out_shape...]
  transfers between devices with their start and end apart: 1 -> 1, of which waited for: 1 -> 1; matrix products, arithmetic and copies ran while one was open for 0% -> 1% of each run, Pallas kernels for 0% -> 0%
where the time goes in v4:
time: 165 us; the launch traced here: 164 us
  Pallas kernels  101 us (61%)
  waiting for transfers between devices  32.8 us (20%)
  between operations  14.2 us (9%)
  local copies, waits for them, and re-layouts  7.7 us (5%)
  matrix products  5.49 us (3%)
  other arithmetic  3.29 us (2%)
    pallas_call x1, Pallas kernels, run_experts(): pl.pallas_call(functools.partial(experts_kernel, n), out_shape=jax.ShapeD...  57.1 us
    pallas_call x1, Pallas kernels, project_hits(): pl.pallas_call(functools.partial(project_kernel, n, blk_count), out_shape...  43.7 us
    reduce_scatter x1, waiting for transfers between devices, body(): lax.psum_scatter(partial_out.astype(jnp.bfloat16), 'exp', scatter_dimensi...  32.7 us
  transfers between devices with their start and end apart: 1, of which 1 were waited for; matrix products, arithmetic and copies ran while one was open for 1% of the time, Pallas kernels for 0%

profile of v4, /device:TPU:0, one launch (start us, length us, event | category | flops | bytes accessed | tf_op | source)
XLA Modules:
  0.0 164.2 jit_solution(16529464780767207449)
XLA Ops:
  7.2 0.0 copy-start
  7.2 0.0 reduce-scatter.2.cloned.1.call-start
  7.2 1.4 broadcast_in_dim.16.gain
  8.6 43.7 %shard_map.140 = (bf16[4,128,384]{2,1,0:T(8,128)(2,1)}, bf16[8,4,128,256]{3,2,1,0:T(8,128)(2,1)}) custom-call(bf16[128,1536]{1,0:T(8,128)(2,1)} %bitcast.45, f32[1,1536]{1,0:T(1,128)} %broadcast_in_dim.16.gain, bf16[1536,384]{1,0:T(8,128)(2,1)} %asking_in.1, bf16[1536,128]{1,0:T(8,128)(2,1)} %lookup_in.1, bf16[1536,128]{1,0:T(8,128)(2,1)} %content_in.1), custom_call_target="tpu_custom_call" | custom-call | tf_op jit(solution)/shard_map/pallas_call | solution.py:199
  52.3 0.0 copy-start.5
  52.3 1.7 %copy.29 = bf16[4,8,128,256]{3,2,1,0:T(8,128)(2,1)S(1)} copy(bf16[4,8,128,256]{3,2,0,1:T(8,128)(2,1)} %bitcast.47) | data formatting | bytes 4194304 | tf_op jit(solution)/shard_map/transpose | solution.py:32
  54.1 1.9 %copy.30 = bf16[4,128,384]{1,2,0:T(8,128)(2,1)} copy(bf16[4,128,384]{2,1,0:T(8,128)(2,1)} %get-tuple-element.5) | data formatting | bytes 786432 | tf_op jit(solution)/shard_map/pallas_call | solution.py:199
  56.0 0.0 copy-done.5
  56.0 0.1 dynamic-slice_multiply_fusion
  56.1 2.0 %bitcast_reduce_fusion = (f32[4,3,128]{2,1,0:T(4,128)S(1)}, f32[4,1024,128,3]{2,1,3,0:T(8,128)S(1)}) fusion(f32[3]{0:T(128)S(1)} %dynamic-slice_multiply_fusion, bf16[4,128,3,128]{1,3,2,0:T(8,128)(2,1)} %bitcast.46, bf16[4,1024,256]{2,1,0:T(8,128)(2,1)S(1)} %bitcast.43), kind=kOutput, calls=%fused_computation | convolution fusion | flops 405797376 | bytes 7739904 | tf_op jit(solution)/shard_map/sigd,sjd->sgij/dot_general | solution.py:35
  58.0 1.3 multiply_reduce_fusion.1
  59.4 0.0 copy-done
  59.4 0.0 copy-start.3
  59.4 0.0 copy-start.4
  59.4 0.0 copy-start.1
  59.4 0.0 copy-start.2
  59.4 2.2 %fusion.2 = bf16[4,128,1536]{2,1,0:T(8,128)(2,1)} fusion(bf16[3,128,1536,1]{2,1,0,3:T(8,128)(2,1)S(1)} %bitcast.42, f32[4,3,128,128]{2,3,1,0:T(8,128)S(1)} %get-tuple-element.9, f32[4,3,128]{2,1,0:T(4,128)S(1)} %add_rsqrt_fusion), kind=kOutput, calls=%fused_computation.6 | convolution fusion | flops 605159424 | bytes 3545088 | tf_op jit(solution)/shard_map/sgid,gde->sie/dot_general | solution.py:43
  61.6 0.0 reduce-scatter.2.cloned.1.call-update
  61.6 0.0 copy-done.3
  61.7 0.0 copy-done.4
  61.7 0.1 select_reduce_fusion
  61.8 0.9 copy.37.gates_ref
  62.6 32.7 %reduce-scatter.2.cloned.1.call-done = bf16[1,128,1536]{2,1,0:T(8,128)(2,1)} async-done(((bf16[4,128,1536]{2,1,0:T(8,128)(2,1)}), bf16[1,128,1536]{2,1,0:T(8,128)(2,1)}) %reduce-scatter.2.cloned.1.call-update) | async-done | bytes 393232 | tf_op jit(solution)/shard_map/reduce_scatter | solution.py:354
  95.4 0.0 copy-done.1
  95.4 1.2 multiply_reduce_fusion
  96.6 0.0 copy-done.2
  96.6 1.9 %fusion.5.x_ref = bf16[128,1536]{1,0:T(8,128)(2,1)} fusion(bf16[1,128,1536]{2,1,0:T(8,128)(2,1)} %reduce-scatter.2.cloned.1.call-done, bf16[1,128,1536]{2,1,0:T(8,128)(2,1)S(1)} %copy-done.1, f32[1536]{0:T(1024)S(1)} %copy-done.2, f32[128]{0:T(128)S(1)} %add_rsqrt_fusion.1), kind=kLoop, calls=%fused_computation.16 | loop fusion | flops 1179648 | bytes 1186304 | tf_op jit(solution)/shard_map/squeeze | solution.py:364
  98.5 57.1 %shard_map.141 = bf16[128,1536]{1,0:T(8,128)(2,1)} custom-call(bf16[128,1536]{1,0:T(8,128)(2,1)} %fusion.5.x_ref, f32[4,128,2]{2,1,0:T(8,128)} %copy.37.gates_ref, bf16[2,1536,384]{2,1,0:T(8,128)(2,1)} %switch_in.1, bf16[2,1536,384]{2,1,0:T(8,128)(2,1)} %widen_in.1, bf16[2,384,1536]{2,1,0:T(8,128)(2,1)} %shrink_in.1), custom_call_target="tpu_custom_call" | custom-call | tf_op jit(solution)/shard_map/pallas_call | solution.py:300
  155.6 1.8 %copy.46 = bf16[1,128,1536]{2,1,0:T(8,128)(2,1)} copy(bf16[1,128,1536]{2,1,0:T(8,128)(2,1)} %bitcast.48) | data formatting | bytes 786432
  (5 shorter events, 0.0 us)
Async XLA Ops:
  7.2 52.2 %copy-start = (bf16[384,1536]{1,0:T(8,128)(2,1)S(1)}, bf16[384,1536]{1,0:T(8,128)(2,1)}, u32[]{:S(2)}) copy-start(bf16[384,1536]{1,0:T(8,128)(2,1)} %param.18) | copy-start | bytes 3538948
  7.2 88.2 %reduce-scatter.2.cloned.1.call-start = ((), (), s32[]{:S(2)}) async-start(), calls=%async_computation.1 | async-start | bytes 1966080 | tf_op jit(solution)/shard_map/reduce_scatter | solution.py:354
  52.3 3.7 %copy-start.5 = (f32[12]{0:T(128)S(1)}, f32[12]{0:T(128)}, u32[]{:S(2)}) copy-start(f32[12]{0:T(128)} %param.19) | copy-start | bytes 148
  59.4 2.3 %copy-start.3 = (s32[4,128,2]{1,2,0:T(2,128)S(1)}, s32[4,128,2]{1,2,0:T(2,128)}, u32[]{:S(2)}) copy-start(s32[4,128,2]{1,2,0:T(2,128)} %param.24) | copy-start | bytes 12292
  59.4 2.3 %copy-start.4 = (f32[4,128,2]{1,2,0:T(2,128)S(1)}, f32[4,128,2]{1,2,0:T(2,128)}, u32[]{:S(2)}) copy-start(f32[4,128,2]{1,2,0:T(2,128)} %param.25) | copy-start | bytes 12292
  59.4 36.0 %copy-start.1 = (bf16[1,128,1536]{2,1,0:T(8,128)(2,1)S(1)}, bf16[1,128,1536]{2,1,0:T(8,128)(2,1)}, u32[]{:S(2)}) copy-start(bf16[1,128,1536]{2,1,0:T(8,128)(2,1)} %param.13) | copy-start | bytes 1179652
  59.4 37.2 %copy-start.2 = (f32[1536]{0:T(1024)S(1)}, f32[1536]{0:T(1024)}, u32[]{:S(2)}) copy-start(f32[1536]{0:T(1024)} %param.20) | copy-start | bytes 18436
Sparse Core Ops, SparseCore 0:
  61.8 33.5 reduce-scatter.1

commit v5 on v4

--- a/solution.py
+++ b/solution.py
@@ -23,24 +23,6 @@
 
 def head_norm(values):
     return values * lax.rsqrt(jnp.mean(values * values, axis=-1, keepdims=True) + 1e-06)
-
-
-def attend_hits(query_heads, pairs, final_projector, logit_multipliers):
-    events, row_count, _ = query_heads.shape
-    lanes = logit_multipliers.shape[0]
-    query_heads = query_heads.reshape(events, row_count, lanes, PER_LANE_DIM)
-    pairs = jnp.swapaxes(pairs, 0, 1).reshape(events, -1, 2 * PER_LANE_DIM)
-    keys, values = pairs[..., :PER_LANE_DIM], pairs[..., PER_LANE_DIM:]
-    scale = logit_multipliers / math.sqrt(PER_LANE_DIM)
-    scores = jnp.einsum("sigd,sjd->sgij", query_heads, keys, preferred_element_type=jnp.float32)
-    expo = jnp.exp(scores * scale[None, :, None, None])
-    totals = jnp.sum(expo, axis=-1)
-    mixture = jnp.einsum(
-        "sgij,sjd->sgid", expo.astype(jnp.bfloat16), values, preferred_element_type=jnp.float32
-    )
-    heads_out = head_norm(mixture / totals[..., None]).astype(jnp.bfloat16)
-    out_blocks = final_projector.reshape(lanes, PER_LANE_DIM, final_projector.shape[1])
-    return jnp.einsum("sgid,gde->sie", heads_out, out_blocks, preferred_element_type=jnp.float32)
 
 
 def gates_of(labels, shares, expert_ids):
@@ -212,6 +194,91 @@
             collective_id=1, has_side_effects=True, vmem_limit_bytes=56 * 2**20
         ),
     )(rows, gain[None], asking, lookup, content)
+
+
+def attend_kernel(
+    n, q_ref, kv_ref, scale_ref, final, x_ref, gain, update_ref, expert_in_ref,
+    parts, back, total, ret_sem, back_sem,
+):
+    me = lax.axis_index("exp")
+    greet_all(n, "exp")
+
+    def block_of(f):
+        pairs = kv_ref[:, f].reshape(-1, 2 * PER_LANE_DIM)
+        keys, values = pairs[:, :PER_LANE_DIM], pairs[:, PER_LANE_DIM:]
+        summed = None
+        for h in range(final.shape[0] // PER_LANE_DIM):
+            lane = slice(h * PER_LANE_DIM, (h + 1) * PER_LANE_DIM)
+            scores = lax.dot_general(
+                q_ref[f, :, lane],
+                keys,
+                (((1,), (1,)), ((), ())),
+                preferred_element_type=jnp.float32,
+            )
+            expo = jnp.exp(scores * scale_ref[h])
+            mixture = jnp.dot(
+                expo.astype(jnp.bfloat16), values, preferred_element_type=jnp.float32
+            ) / jnp.sum(expo, axis=-1, keepdims=True)
+            term = jnp.dot(
+                head_norm(mixture).astype(jnp.bfloat16),
+                final[lane, :],
+                preferred_element_type=jnp.float32,
+            )
+            summed = term if summed is None else summed + term
+        return summed
+
+    def returned(f):
+        return copy_to(parts.at[f], back.at[f], ret_sem.at[f], back_sem.at[f], exp=f)
+
+    @pl.loop(1, n)
+    def _(k):
+        f = lax.rem(me + k, n)
+        parts[f] = block_of(f).astype(jnp.bfloat16)
+        copy_to(parts.at[f], back.at[me], ret_sem.at[f], back_sem.at[me], exp=f).start()
+
+    total[...] = block_of(me)
+
+    @pl.loop(1, n)
+    def _(k):
+        f = lax.rem(me + k, n)
+        returned(f).wait_recv()
+        total[...] += back[f].astype(jnp.float32)
+
+    update_ref[...] = total[...].astype(jnp.bfloat16)
+    residual = x_ref[...].astype(jnp.float32) + total[...]
+    expert_in_ref[...] = norm_rows(residual, gain[...]).astype(jnp.bfloat16)
+
+    @pl.loop(1, n)
+    def _(k):
+        returned(lax.rem(me + k, n)).wait_send()
+
+
+def attend_hits(query_heads, pairs, logit_multipliers, final_projector, rows, gain):
+    n = lax.axis_size("exp")
+    vmem = pl.BlockSpec(memory_space=pltpu.VMEM)
+    shape = jax.ShapeDtypeStruct(rows.shape, jnp.bfloat16)
+    return pl.pallas_call(
+        functools.partial(attend_kernel, n),
+        out_shape=(shape, shape),
+        in_specs=[vmem, vmem, pl.BlockSpec(memory_space=pltpu.SMEM), vmem, vmem, vmem],
+        out_specs=(vmem, vmem),
+        scratch_shapes=[
+            pltpu.VMEM((n, *rows.shape), jnp.bfloat16),
+            pltpu.VMEM((n, *rows.shape), jnp.bfloat16),
+            pltpu.VMEM(rows.shape, jnp.float32),
+        ]
+        + [pltpu.SemaphoreType.DMA((n,))] * 2,
+        compiler_params=pltpu.CompilerParams(
+            collective_id=3, has_side_effects=True, vmem_limit_bytes=56 * 2**20
+        ),
+    )(
+        query_heads,
+        pairs,
+        logit_multipliers / math.sqrt(PER_LANE_DIM),
+        final_projector,
+        rows,
+        gain[None],
+    )
 
 
 def experts_kernel(
@@ -345,29 +412,25 @@
     device_scratch = lax.dynamic_slice_in_dim(
         logit_multipliers, specialist_slot * local_lane_count, local_lane_count
     )
-    partial_out = attend_hits(
+    attention_update, expert_in = attend_hits(
         query_heads,
         pairs,
+        device_scratch,
         final_projector,
-        device_scratch,
-    )
-    attention_full = lax.psum_scatter(
-        partial_out.astype(jnp.bfloat16), "exp", scatter_dimension=0, tiled=True
-    ).astype(jnp.float32)
-    attention_update = attention_full.astype(jnp.bfloat16)
-    residual = residual_deposit_sequence.astype(jnp.float32) + attention_full
-    expert_in = norm_rows(residual, premixture_rescaler).astype(jnp.bfloat16)
+        residual_deposit_sequence[0],
+        premixture_rescaler,
+    )
     local_experts = specialist_switch_tensor.shape[0]
     expert_ids = specialist_slot * local_experts + jnp.arange(local_experts, dtype=jnp.int32)
     gates = gates_of(picked_specialist_labels, specialist_shares, expert_ids)
     expert_update = run_experts(
-        expert_in[0],
+        expert_in,
         gates,
         specialist_switch_tensor,
         specialist_widen_tensor,
         specialist_shrink_tensor,
     )[None]
-    return (attention_update, expert_update)
+    return (attention_update[None], expert_update)
 
 
 def solution(mesh):

time: 165 us -> 152 us (0.921)
  Pallas kernels: 101 us -> 145 us
  waiting for transfers between devices: 32.8 us -> 0 us
  between operations: 14.2 us -> 0.74 us
  matrix products: 5.49 us -> 0 us
  local copies, waits for them, and re-layouts: 7.7 us -> 5.3 us
  other arithmetic: 3.29 us -> 1.33 us
    pallas_call x0 -> x1, Pallas kernels: none -> 35.4 us  [attend_hits(): pl.pallas_call(functools.partial(attend_kernel, n), out_shape=(shape, sha...]
    reduce_scatter x1 -> x0, waiting for transfers between devices: 32.7 us -> none  [body(): lax.psum_scatter(partial_out.astype(jnp.bfloat16), 'exp', scatter_dimensi...]
    pallas_call x1, Pallas kernels: 57.1 us -> 65.5 us  [run_experts(): pl.pallas_call(functools.partial(experts_kernel, n), out_shape=jax.ShapeD...]
    dot_general x3 -> x0, matrix products: 5.49 us -> none  [the longest x1 2.18 us: attend_hits(): jnp.einsum('sgid,gde->sie', heads_out, out_blocks, preferred_element_type...]
    pallas_call x1 -> x0, local copies, waits for them, and re-layouts: 1.91 us -> none  [project_hits(): pl.pallas_call(functools.partial(project_kernel, n, blk_count), out_shape...]
    squeeze x1 -> x0, other arithmetic: 1.9 us -> none  [body(): expert_in[0]]
    transpose x1 -> x0, local copies, waits for them, and re-layouts: 1.73 us -> none  [attend_hits(): pairs = jnp.swapaxes(pairs, 0, 1).reshape(events, -1, 2 * PER_LANE_DIM)]
  transfers between devices with their start and end apart: 1 -> 0, of which waited for: 1 -> 0; matrix products, arithmetic and copies ran while one was open for 1% -> 0% of each run, Pallas kernels for 0% -> 0%
where the time goes in v5:
time: 152 us
  Pallas kernels  145 us (95%)
  local copies, waits for them, and re-layouts  5.3 us (3%)
    pallas_call x1, Pallas kernels, run_experts(): pl.pallas_call(functools.partial(experts_kernel, n), out_shape=jax.ShapeD...  65.5 us
    pallas_call x1, Pallas kernels, project_hits(): pl.pallas_call(functools.partial(project_kernel, n, blk_count), out_shape...  43.7 us
    pallas_call x1, Pallas kernels, attend_hits(): pl.pallas_call(functools.partial(attend_kernel, n), out_shape=(shape, sha...  35.4 us

profile of v5, /device:TPU:0, one launch (start us, length us, event | category | flops | bytes accessed | tf_op | source)
XLA Modules:
  0.0 152.0 jit_solution(7916603346581248298)
XLA Ops:
  0.6 0.0 copy-start.1
  0.6 1.2 dynamic-slice_multiply_fusion.scale_ref
  1.9 1.3 broadcast_in_dim.26.gain
  3.2 43.7 %shard_map.140 = (bf16[4,128,384]{2,1,0:T(8,128)(2,1)}, bf16[8,4,128,256]{3,2,1,0:T(8,128)(2,1)}) custom-call(bf16[128,1536]{1,0:T(8,128)(2,1)} %bitcast.4, f32[1,1536]{1,0:T(1,128)} %broadcast_in_dim.26.gain, bf16[1536,384]{1,0:T(8,128)(2,1)} %asking_in.1, bf16[1536,128]{1,0:T(8,128)(2,1)} %lookup_in.1, bf16[1536,128]{1,0:T(8,128)(2,1)} %content_in.1), custom_call_target="tpu_custom_call" | custom-call | tf_op jit(solution)/shard_map/pallas_call | solution.py:181
  46.9 0.0 copy-start.2
  46.9 0.0 copy-start.3
  46.9 0.0 copy-done.1
  46.9 0.6 broadcast_in_dim.27.gain
  47.5 35.4 %shard_map.141 = (bf16[128,1536]{1,0:T(8,128)(2,1)}, bf16[128,1536]{1,0:T(8,128)(2,1)}) custom-call(bf16[4,128,384]{2,1,0:T(8,128)(2,1)} %get-tuple-element.6.q_ref, bf16[8,4,128,256]{3,2,1,0:T(8,128)(2,1)} %get-tuple-element.7.kv_ref, f32[3]{0:T(128)} %dynamic-slice_multiply_fusion.scale_ref, bf16[384,1536]{1,0:T(8,128)(2,1)} %final.1, ...), custom_call_target="tpu_custom_call" | custom-call | tf_op jit(solution)/shard_map/pallas_call | solution.py:260
  82.9 0.0 copy-done.2
  82.9 0.0 copy-done.3
  82.9 0.1 select_reduce_fusion
  83.0 0.9 copy.19.gates_ref
  83.9 0.0 copy-start
  83.9 65.5 %shard_map.142 = bf16[128,1536]{1,0:T(8,128)(2,1)} custom-call(bf16[128,1536]{1,0:T(8,128)(2,1)} %get-tuple-element.9.x_ref, f32[4,128,2]{2,1,0:T(8,128)} %copy.19.gates_ref, bf16[2,1536,384]{2,1,0:T(8,128)(2,1)} %switch_in.1, bf16[2,1536,384]{2,1,0:T(8,128)(2,1)} %widen_in.1, bf16[2,384,1536]{2,1,0:T(8,128)(2,1)} %shrink_in.1), custom_call_target="tpu_custom_call" | custom-call | tf_op jit(solution)/shard_map/pallas_call | solution.py:367
  149.4 0.0 copy-done
  149.5 0.7 copy.22
  150.2 1.8 %copy.23 = bf16[1,128,1536]{2,1,0:T(8,128)(2,1)} copy(bf16[1,128,1536]{2,1,0:T(8,128)(2,1)} %bitcast.3) | data formatting | bytes 786432
  (3 shorter events, 0.0 us)
Async XLA Ops:
  0.6 46.3 %copy-start.1 = (f32[1536]{0:T(1024)S(1)}, f32[1536]{0:T(1024)}, u32[]{:S(2)}) copy-start(f32[1536]{0:T(1024)} %param.20) | copy-start | bytes 18436
  46.9 36.0 %copy-start.2 = (s32[4,128,2]{1,2,0:T(2,128)S(1)}, s32[4,128,2]{1,2,0:T(2,128)}, u32[]{:S(2)}) copy-start(s32[4,128,2]{1,2,0:T(2,128)} %param.24) | copy-start | bytes 12292
  46.9 36.0 %copy-start.3 = (f32[4,128,2]{1,2,0:T(2,128)S(1)}, f32[4,128,2]{1,2,0:T(2,128)}, u32[]{:S(2)}) copy-start(f32[4,128,2]{1,2,0:T(2,128)} %param.25) | copy-start | bytes 12292
  83.9 65.6 %copy-start = (bf16[128,1536]{1,0:T(8,128)(2,1)S(1)}, bf16[128,1536]{1,0:T(8,128)(2,1)}, u32[]{:S(2)}) copy-start(bf16[128,1536]{1,0:T(8,128)(2,1)} %get-tuple-element.8) | copy-start | bytes 1179652
